TPU v7x, 512 devices: a whole 4x8x8 slice. The times are simulated.
512 devices in a mesh: elem: 128 (over x_hi, z, y), lev: 4 (over x_lo, core).
Axes of the slice: x: 4 (x_hi: 2, x_lo: 2; x = x_hi * 2 + x_lo), y: 8, z: 8, core: 2. Of those that a mesh axis runs over, the one named last changes fastest.
Arguments:
- thermal_anomaly: float32 [72, 16, 65536], P('lev', None, 'elem'), may hold values from -6 to 6
- zonal_velocity: bfloat16 [72, 16, 65536], P('lev', None, 'elem'), may hold values from -6 to 6
- meridional_velocity: bfloat16 [72, 16, 65536], P('lev', None, 'elem'), may hold values from -6 to 6
- patch_mesh_position: int32 [128, 512], P('elem'), may hold values from 0 to 511, each once within a row
- sunlit_mask: int32 [65536], P('elem'), may hold values from 0 to 1, as said below
- entry_matrix: bfloat16 [512, 72], replicated, may hold values from -0.75 to 0.75
- entry_offset: float32 [512], replicated, may hold values from -6 to 6
- inner_matrices: bfloat16 [2, 512, 512], replicated, may hold values from -0.25 to 0.25
- inner_offsets: float32 [2, 512], replicated, may hold values from -6 to 6
- readout_matrix: bfloat16 [72, 512], replicated, may hold values from -0.25 to 0.25
Outputs:
- temperature_out: float32 [72, 16, 65536], P('lev', None, 'elem')
Inputs may be any that keep to these rules, and one draw needn't show every extreme that they name: `sunlit_mask`: the flags of element e and of element e + 32768 sum to one. `patch_mesh_position`: each row is an ordering of the 512 grid slots of one device.
All inputs are finite; a program needn't handle non-finite values.
Results may differ from a plain program's by a relative error of at most 0.0028.
Values may be sent and summed in bfloat16 or wider, within the bound.
A program may use at most 64 MiB of HBM per device.

v0:
```python
import math

import jax
import jax.numpy as jnp
from jax import lax
from jax.sharding import PartitionSpec as P

ELEMENTS_FIRST = 8
ELEMENTS_SECOND = 64


def extended(shard, sides, width):
    for axis, dim in sides:
        count, length = (lax.axis_size(axis), shard.shape[dim])
        up = [(i, (i + 1) % count) for i in range(count)]
        down = [(j, i) for i, j in up]
        last = lax.slice_in_dim(shard, length - width, length, axis=dim)
        first = lax.slice_in_dim(shard, 0, width, axis=dim)
        before = lax.ppermute(last, axis, up)
        after = lax.ppermute(first, axis, down)
        shard = jnp.concatenate([before, shard, after], axis=dim)
    return shard


def from_partner(block, axis, bit):
    count = lax.axis_size(axis)
    route = []
    for low in range(count):
        high = low | 1 << bit
        if high != low and high < count:
            route += [(low, high), (high, low)]
    return lax.ppermute(block, axis, route)


def derivative_table():
    gll_nodes = [-1.0, -1.0 / math.sqrt(5.0), 1.0 / math.sqrt(5.0), 1.0]
    table_rows = []
    for i in range(4):
        one_row = []
        for j in range(4):
            if i == j:
                entry_value = sum((1.0 / (gll_nodes[i] - gll_nodes[m]) for m in range(4) if m != i))
            else:
                upper_part = 1.0
                lower_part = 1.0
                for m in range(4):
                    if m != i and m != j:
                        upper_part = upper_part * (gll_nodes[i] - gll_nodes[m])
                    if m != j:
                        lower_part = lower_part * (gll_nodes[j] - gll_nodes[m])
                entry_value = upper_part / lower_part
            one_row.append(entry_value)
        table_rows.append(one_row)
    return jnp.array(table_rows, jnp.float32)


def along_first(table, field):
    return jnp.einsum("ik,lkjxy->lijxy", table, field, precision=lax.Precision.HIGHEST)


def along_second(table, field):
    return jnp.einsum("jk,likxy->lijxy", table, field, precision=lax.Precision.HIGHEST)


def compute_rate_change(temp_grid, wind_u, wind_v):
    table = derivative_table()
    grad_x = along_first(table, temp_grid)
    grad_y = along_second(table, temp_grid)
    curve = along_first(table, grad_x) + along_second(table, grad_y)
    return -(wind_u * grad_x + wind_v * grad_y) + 0.1 * curve


def mean_along_abscissa(field):
    upper = field[:, 3]
    lower_local = field[:, 0]
    edges = jnp.stack([lower_local[:, :, 0, :], upper[:, :, -1, :]], axis=2)
    padded = extended(edges, (("elem", 2),), 1)
    from_prev = padded[:, :, 0, :]
    from_next = padded[:, :, 3, :]
    lower_next = jnp.concatenate([lower_local[:, :, 1:, :], from_next[:, :, None, :]], axis=2)
    middle = (upper + lower_next) * 0.5
    first_middle = (from_prev + lower_local[:, :, 0, :]) * 0.5
    new_lower = jnp.concatenate([first_middle[:, :, None, :], middle[:, :, :-1, :]], axis=2)
    return jnp.stack([new_lower, field[:, 1], field[:, 2], middle], axis=1)


def mean_along_ordinate(field):
    upper = field[:, :, 3]
    lower = jnp.roll(field[:, :, 0], -1, axis=3)
    middle = (upper + lower) * 0.5
    return field.at[:, :, 3].set(middle).at[:, :, 0].set(jnp.roll(middle, 1, axis=3))


def radiate(column, entry_matrix, entry_offset, inner_matrices, inner_offsets, readout_matrix):
    neural_layer_number, quadrature_abscissae, summed_quantity = column.shape
    flat = column.reshape(neural_layer_number, quadrature_abscissae * summed_quantity)
    hidden = jax.nn.silu(
        jnp.dot(entry_matrix, flat, preferred_element_type=jnp.float32) + entry_offset[:, None]
    ).astype(jnp.bfloat16)
    for m in range(inner_matrices.shape[0]):
        hidden = jax.nn.silu(
            jnp.dot(inner_matrices[m], hidden, preferred_element_type=jnp.float32)
            + inner_offsets[m][:, None]
        ).astype(jnp.bfloat16)
    heat = jnp.dot(readout_matrix, hidden, preferred_element_type=jnp.float32)
    return heat.reshape(readout_matrix.shape[0], quadrature_abscissae, summed_quantity)


def physics(
    column, flags, entry_matrix, entry_offset, inner_matrices, inner_offsets, readout_matrix
):
    summed_quantity = column.shape[2]
    half = summed_quantity // 2
    lower = lax.axis_index("elem") < lax.axis_size("elem") // 2
    partner_bit = lax.axis_size("elem").bit_length() - 2
    mine = jnp.where(lower, column[:, :, :half], column[:, :, half:])
    other = jnp.where(lower, column[:, :, half:], column[:, :, :half])
    mine_flags = jnp.where(lower, flags[:half], flags[half:])
    arrived = from_partner(other, "elem", partner_bit)
    chosen = jnp.where((mine_flags == 1)[None, None, :], mine, arrived)
    heat = radiate(
        chosen, entry_matrix, entry_offset, inner_matrices, inner_offsets, readout_matrix
    )
    share = mine_flags.astype(jnp.float32)[None, None, :]
    kept = (heat * share).astype(jnp.bfloat16)
    given = (heat * (1.0 - share)).astype(jnp.bfloat16)
    returned = from_partner(given, "elem", partner_bit)
    first_out = jnp.where(lower, kept, returned)
    second_out = jnp.where(lower, returned, kept)
    return jnp.concatenate([first_out, second_out], axis=2)


def on_device(
    thermal_anomaly,
    zonal_velocity,
    meridional_velocity,
    patch_mesh_position,
    sunlit_mask,
    entry_matrix,
    entry_offset,
    inner_matrices,
    inner_offsets,
    readout_matrix,
):
    neural_layer_number, quadrature_abscissae, summed_quantity = thermal_anomaly.shape
    slots = patch_mesh_position[0]
    patch_permutation_map = (
        jnp.zeros((summed_quantity,), jnp.int32)
        .at[slots]
        .set(jnp.arange(summed_quantity, dtype=jnp.int32))
    )
    mesh_thermal_anomaly = jnp.take(thermal_anomaly, patch_permutation_map, axis=2).reshape(
        neural_layer_number, 4, 4, ELEMENTS_FIRST, ELEMENTS_SECOND
    )
    mesh_zonal_velocity = (
        jnp.take(zonal_velocity, patch_permutation_map, axis=2)
        .astype(jnp.float32)
        .reshape(neural_layer_number, 4, 4, ELEMENTS_FIRST, ELEMENTS_SECOND)
    )
    mesh_meridional_velocity = (
        jnp.take(meridional_velocity, patch_permutation_map, axis=2)
        .astype(jnp.float32)
        .reshape(neural_layer_number, 4, 4, ELEMENTS_FIRST, ELEMENTS_SECOND)
    )
    rate_change = mean_along_ordinate(
        mean_along_abscissa(
            compute_rate_change(mesh_thermal_anomaly, mesh_zonal_velocity, mesh_meridional_velocity)
        )
    )
    marched_mesh = (mesh_thermal_anomaly + 0.05 * rate_change).reshape(
        neural_layer_number, quadrature_abscissae, summed_quantity
    )
    advance_timestep = jnp.take(marched_mesh, slots, axis=2)
    column = advance_timestep.astype(jnp.bfloat16)
    gathered = lax.all_to_all(column, "lev", split_axis=2, concat_axis=0, tiled=True)
    block = gathered.shape[2]
    start = lax.axis_index("lev") * block
    flags_here = lax.dynamic_slice_in_dim(sunlit_mask, start, block)
    heating = physics(
        gathered,
        flags_here,
        entry_matrix,
        entry_offset,
        inner_matrices,
        inner_offsets,
        readout_matrix,
    )
    heating = lax.all_to_all(heating, "lev", split_axis=0, concat_axis=2, tiled=True)
    return advance_timestep + heating.astype(jnp.float32)


def solution(mesh):
    in_specs = (
        P("lev", None, "elem"),
        P("lev", None, "elem"),
        P("lev", None, "elem"),
        P("elem", None),
        P("elem"),
        P(),
        P(),
        P(),
        P(),
        P(),
    )
    out_specs = P("lev", None, "elem")
    return jax.shard_map(
        on_device, mesh=mesh, in_specs=in_specs, out_specs=out_specs, check_vma=False
    )
```

profile of v0, /device:TPU:1, one launch (start us, length us, event | category | flops | bytes accessed | tf_op | source)
XLA Modules:
  0.0 190.0 jit_solution(13986819759635220668)
XLA Ops:
  0.0 0.7 compare_select_fusion
  0.7 2.4 %scatter_custom_fusion = s32[512]{0:T(512)S(1)} fusion(s32[512]{0:T(512)S(1)} %bitcast.176, s32[512]{0:T(512)S(1)} %iota.3, s32[]{:T(128)} %constant.97.clone.1), kind=kCustom, calls=%fused_computation.80 | custom fusion | bytes 2052 | tf_op jit(solution)/shard_map/scatter | solution.py:150
  3.2 4.7 %copy.56 = f32[18,16,512]{0,1,2:T(8,128)} copy(f32[18,16,512]{2,1,0:T(8,128)} %param.19) | data formatting | bytes 1179648 | tf_op args[0]
  7.9 5.2 %gather_fusion = f32[512,18,16]{1,2,0:T(8,128)} fusion(f32[18,16,512]{0,1,2:T(8,128)} %copy.56, s32[1024]{0:T(1024)S(1)} %pad_clamp_fusion.1), kind=kCustom, calls=%fused_computation.clone | custom fusion | bytes 1181696 | tf_op jit(solution)/shard_map/jit(_take)/gather | solution.py:152
  13.0 4.6 %broadcast_select_fusion = f32[512,18,16]{1,2,0:T(8,128)} fusion(f32[512,18,16]{1,2,0:T(8,128)} %gather_fusion, pred[512]{0:T(512)(128)(4,1)S(1)} %compare_and_fusion.1), kind=kLoop, calls=%fused_computation.22 | loop fusion | flops 147456 | bytes 1180160 | tf_op jit(solution)/shard_map/jit(_take)/select_n | solution.py:152
  17.7 3.9 %copy.64 = f32[18,4,4,8,64]{4,2,3,1,0:T(4,128)S(1)} copy(f32[18,4,4,8,64]{0,2,1,4,3:T(4,128)} %bitcast.159) | data formatting | bytes 1179648 | tf_op jit(solution)/shard_map/reshape | solution.py:152
  21.6 5.1 %copy.60 = f32[18,4,4,8,64]{4,1,3,2,0:T(4,128)} copy(f32[18,4,4,8,64]{0,2,1,4,3:T(4,128)} %bitcast.160) | data formatting | bytes 1179648 | tf_op jit(solution)/shard_map/reshape | solution.py:152
  26.7 2.1 %fusion.47 = f32[18,4,8,64,4]{3,4,2,1,0:T(4,128)S(1)} fusion(f32[18,4,4,8,64]{4,2,3,1,0:T(4,128)S(1)} %copy.64, f32[4,4,1,1,1]{1,0,4,3,2:T(4,128)S(1)} %copy-done.6), kind=kOutput, calls=%fused_computation.96 | convolution fusion | flops 7077888 | bytes 1179712 | tf_op jit(solution)/shard_map/jk,likxy->lijxy/dot_general | solution.py:62
  28.9 0.1 copy.105
  29.0 3.3 %fusion.15 = f32[18,4,8,64,4]{3,4,2,1,0:T(4,128)} fusion(f32[4,4,1,1,1]{1,0,4,3,2:T(4,128)S(1)} %copy-done.6, f32[18,4,4,8,64]{4,3,2,1,0:T(8,128)S(1)} %bitcast.167), kind=kOutput, calls=%fused_computation.31 | convolution fusion | flops 7077888 | bytes 1179712 | tf_op jit(solution)/shard_map/jk,likxy->lijxy/dot_general | solution.py:62
  32.3 2.1 %fusion.46 = f32[18,4,8,64,4]{3,4,2,1,0:T(4,128)S(1)} fusion(f32[18,4,4,8,64]{4,1,3,2,0:T(4,128)S(1)} %copy-done.3, f32[4,4,1,1,1]{1,0,4,3,2:T(4,128)S(1)} %copy-done.6), kind=kOutput, calls=%fused_computation.95 | convolution fusion | flops 7077888 | bytes 1179712 | tf_op jit(solution)/shard_map/ik,lkjxy->lijxy/dot_general | solution.py:58
  34.4 0.1 copy.106
  34.6 3.8 %fusion.17 = f32[18,4,8,64,4]{3,4,2,1,0:T(4,128)} fusion(f32[4,4,1,1,1]{1,0,4,3,2:T(4,128)S(1)} %copy-done.6, f32[18,4,4,8,64]{4,3,2,1,0:T(8,128)S(1)} %bitcast.166), kind=kOutput, calls=%fused_computation.33 | convolution fusion | flops 7077888 | bytes 1179712 | tf_op jit(solution)/shard_map/ik,lkjxy->lijxy/dot_general | solution.py:58
  38.4 2.9 %copy.58 = bf16[18,16,512]{0,1,2:T(8,128)(2,1)} copy(bf16[18,16,512]{2,1,0:T(8,128)(2,1)S(1)} %copy-done.4) | data formatting | bytes 589824 | tf_op args[1]
  41.3 3.9 %gather_fusion.1 = bf16[512,18,16]{1,2,0:T(8,128)(2,1)} fusion(bf16[18,16,512]{0,1,2:T(8,128)(2,1)} %copy.58, s32[1024]{0:T(1024)S(1)} %pad_clamp_fusion.1), kind=kCustom, calls=%fused_computation.1.clone | custom fusion | bytes 591872 | tf_op jit(solution)/shard_map/jit(_take)/gather | solution.py:156
  45.3 2.9 %copy.59 = bf16[512,18,16]{0,2,1:T(8,128)(2,1)S(1)} copy(bf16[512,18,16]{1,2,0:T(8,128)(2,1)} %gather_fusion.1) | data formatting | bytes 589824 | tf_op jit(solution)/shard_map/jit(_take)/gather | solution.py:156
  48.2 3.2 %copy.62 = bf16[18,16,512]{0,1,2:T(8,128)(2,1)} copy(bf16[18,16,512]{2,1,0:T(8,128)(2,1)S(1)} %copy-done.5) | data formatting | bytes 589824 | tf_op args[2]
  51.4 4.0 %gather_fusion.2 = bf16[512,18,16]{1,2,0:T(8,128)(2,1)} fusion(bf16[18,16,512]{0,1,2:T(8,128)(2,1)} %copy.62, s32[1024]{0:T(1024)S(1)} %pad_clamp_fusion.1), kind=kCustom, calls=%fused_computation.3.clone | custom fusion | bytes 591872 | tf_op jit(solution)/shard_map/jit(_take)/gather | solution.py:161
  55.4 3.5 %copy.63 = bf16[512,18,16]{0,2,1:T(8,128)(2,1)} copy(bf16[512,18,16]{1,2,0:T(8,128)(2,1)} %gather_fusion.2) | data formatting | bytes 589824 | tf_op jit(solution)/shard_map/jit(_take)/gather | solution.py:161
  58.9 1.9 bitcast_convert_fusion.2
  60.8 2.4 %reshape.169 = f32[18,4,4,8,64]{4,3,2,1,0:T(8,128)} reshape(f32[18,16,512]{2,1,0:T(8,128)} %get-tuple-element.48) | data formatting | bytes 1179648 | tf_op jit(solution)/shard_map/reshape | solution.py:163
  63.1 1.3 reshape.167
  64.4 3.0 %fusion.14 = f32[18,4,4,8,64]{4,3,2,1,0:T(8,128)S(1)} fusion(f32[18,4,8,64,4]{3,4,2,1,0:T(4,128)} %fusion.15, f32[18,4,8,64,4]{3,4,2,1,0:T(4,128)} %fusion.17, f32[18,4,4,8,64]{4,3,2,1,0:T(8,128)} %reshape.169, f32[18,4,4,8,64]{4,3,2,1,0:T(8,128)} %reshape.167, f32[18,4,8,64,4]{3,4,2,1,0:T(4,128)S(1)} %fusion.46, f32[18,4,8,64,4]{3,4,2,1,0:T(4,128)S(1)} %fusion.47), kind=kLoop, calls=%fused_computation.30 | loop fusion | flops 1032192 | bytes 4128768 | tf_op jit(solution)/shard_map/add | solution.py:70
  67.4 1.0 copy-done.1
  68.5 4.0 %collective-permute-start = (f32[18,4,1,64]{3,2,1,0:T(1,128)S(1)}, f32[18,4,1,64]{3,2,1,0:T(1,128)S(1)}, u32[]{:S(2)}, u32[]{:S(2)}) collective-permute-start(f32[18,4,1,64]{3,2,1,0:T(1,128)S(1)} %slice.162), channel_id=1, source_target_pairs={{0,4},{4,8},{8,12},{12,16},{16,20},{20,24},{24,28},{28,32},{32,36}... | collective-permute-start | bytes 55304 | tf_op jit(solution)/shard_map/ppermute | solution.py:19
  72.7 0.8 dynamic_slice.3
  73.6 13.2 %collective-permute-done = f32[18,4,1,64]{3,2,1,0:T(1,128)S(1)} collective-permute-done((f32[18,4,1,64]{3,2,1,0:T(1,128)S(1)}, f32[18,4,1,64]{3,2,1,0:T(1,128)S(1)}, u32[]{:S(2)}, u32[]{:S(2)}) %collective-permute-start) | collective-permute-done | bytes 18464 | tf_op jit(solution)/shard_map/ppermute | solution.py:19
  86.8 3.4 %collective-permute-start.1 = (f32[18,4,1,64]{3,2,1,0:T(1,128)S(1)}, f32[18,4,1,64]{3,2,1,0:T(1,128)S(1)}, u32[]{:S(2)}, u32[]{:S(2)}) collective-permute-start(f32[18,4,1,64]{3,2,1,0:T(1,128)S(1)} %get-tuple-element.42), channel_id=1, source_target_pairs={{4,0},{8,4},{12,8},{16,12},{20,16},{24,20},{28,24},{32,28},{36,32}... | collective-permute-start | bytes 55304 | tf_op jit(solution)/shard_map/ppermute | solution.py:20
  90.2 3.9 %copy.85 = f32[18,4,4,8,64]{4,3,2,1,0:T(8,128)S(1)} copy(f32[18,4,4,8,64]{0,2,1,4,3:T(4,128)} %bitcast.161) | data formatting | bytes 1179648 | tf_op jit(solution)/shard_map/reshape | solution.py:152
  94.1 1.3 copy-done.2
  95.7 0.8 slice-done
  96.4 0.1 pad_maximum_fusion
  96.6 0.8 fusion.41
  97.4 0.9 fusion.42
  98.2 0.3 copy.77
  98.6 1.1 fusion.34
  99.7 1.1 copy.78
  100.7 0.1 slice.172
  100.9 1.2 fusion.33
  102.1 0.1 fusion.35
  102.3 1.3 multiply_add_fusion
  103.6 4.9 %copy.88 = f32[18,4,4,8,64]{0,2,1,4,3:T(4,128)} copy(f32[18,4,4,8,64]{4,3,2,1,0:T(8,128)} %multiply_add_fusion) | data formatting | bytes 1179648 | tf_op jit(solution)/shard_map/reshape | solution.py:170
  108.5 5.1 %gather_fusion.3 = f32[512,18,16]{1,2,0:T(8,128)} fusion(f32[18,16,512]{0,1,2:T(8,128)} %bitcast.165, s32[1024]{0:T(1024)S(1)} %pad_clamp_fusion), kind=kCustom, calls=%fused_computation.2.clone | custom fusion | bytes 1181696 | tf_op jit(solution)/shard_map/jit(_take)/gather | solution.py:173
  113.6 3.3 %fusion.45 = bf16[512,16,18]{2,1,0:T(8,128)(2,1)S(1)} fusion(f32[512,18,16]{1,2,0:T(8,128)} %gather_fusion.3, pred[512]{0:T(512)(128)(4,1)S(1)} %compare_and_fusion), kind=kLoop, calls=%fused_computation.94 | loop fusion | flops 147456 | bytes 885248
  116.9 4.6 %reshape.229 = bf16[4,2,18432]{2,1,0:T(2,128)(2,1)} reshape(bf16[512,16,18]{2,1,0:T(8,128)(2,1)S(1)} %fusion.45) | data formatting | bytes 589824
  121.5 5.5 %all-to-all-start = ((bf16[4,2,18432]{2,1,0:T(2,128)(2,1)}), bf16[4,2,18432]{2,1,0:T(2,128)(2,1)S(1)}, u32[]{:S(2)}, u32[]{:S(2)}) async-start(bf16[4,2,18432]{2,1,0:T(2,128)(2,1)} %reshape.229), calls=%async_computation | async-start | bytes 589824 | tf_op jit(solution)/shard_map/all_to_all | solution.py:175
  127.0 5.5 %all-to-all-done = bf16[4,2,18432]{2,1,0:T(2,128)(2,1)S(1)} async-done(((bf16[4,2,18432]{2,1,0:T(2,128)(2,1)}), bf16[4,2,18432]{2,1,0:T(2,128)(2,1)S(1)}, u32[]{:S(2)}, u32[]{:S(2)}) %all-to-all-start) | async-done | bytes 294944 | tf_op jit(solution)/shard_map/all_to_all | solution.py:175
  132.6 5.2 %reshape.230 = bf16[512,16,18]{2,1,0:T(8,128)(2,1)S(1)} reshape(bf16[4,2,18432]{2,1,0:T(2,128)(2,1)S(1)} %all-to-all-done) | data formatting | bytes 589824
  137.8 1.9 copy.81
  139.7 0.1 broadcast_select_fusion.3
  139.8 2.1 %collective-permute-start.2 = (bf16[72,16,64]{2,1,0:T(8,128)(2,1)S(1)}, bf16[72,16,64]{2,1,0:T(8,128)(2,1)S(1)}, u32[]{:S(2)}, u32[]{:S(2)}) collective-permute-start(bf16[72,16,64]{2,1,0:T(8,128)(2,1)S(1)} %broadcast_select_fusion.3), channel_id=1, source_target_pairs={{0,256},{256,0},{4,260},{260,4},{8,264},{264,8},{12,268},{268,12},... | collective-permute-start | bytes 442376 | tf_op jit(solution)/shard_map/ppermute | solution.py:32
  141.9 9.1 %collective-permute-done.2 = bf16[72,16,64]{2,1,0:T(8,128)(2,1)S(1)} collective-permute-done((bf16[72,16,64]{2,1,0:T(8,128)(2,1)S(1)}, bf16[72,16,64]{2,1,0:T(8,128)(2,1)S(1)}, u32[]{:S(2)}, u32[]{:S(2)}) %collective-permute-start.2) | collective-permute-done | bytes 147488 | tf_op jit(solution)/shard_map/ppermute | solution.py:32
  151.0 0.1 select_select_fusion
  151.2 0.2 reshape.164
  151.4 2.5 %fusion.10 = bf16[512,1024]{0,1:T(8,128)(2,1)} fusion(f32[512]{0:T(512)S(1)} %bitcast.178, bf16[72,1024]{1,0:T(8,128)(2,1)S(1)} %reshape.164, bf16[512,72]{0,1:T(8,128)(2,1)S(1)} %copy-done, f32[512]{0:T(512)S(1)} %copy-done.11, bf16[2,512,512]{2,1,0:T(8,128)(2,1)S(1)} %copy-done.9), kind=kOutput, calls=%fused_computation.24 | convolution fusion | flops 618659840 | bytes 1798144 | tf_op jit(solution)/shard_map/dot_general | solution.py:102
  153.9 2.5 %fusion.19 = f32[72,1024]{1,0:T(8,128)S(1)} fusion(bf16[72,512]{1,0:T(8,128)(2,1)S(1)} %copy-done.10, bf16[512,1024]{0,1:T(8,128)(2,1)} %fusion.10, f32[512]{0:T(512)S(1)} %bitcast.177, bf16[2,512,512]{2,1,0:T(8,128)(2,1)S(1)} %copy-done.9), kind=kOutput, calls=%fused_computation.38 | convolution fusion | flops 615514112 | bytes 1943552 | tf_op jit(solution)/shard_map/dot_general | solution.py:105
  156.4 0.1 reshape.165
  156.6 1.9 %collective-permute-start.3 = (bf16[72,16,64]{2,1,0:T(8,128)(2,1)S(1)}, bf16[72,16,64]{2,1,0:T(8,128)(2,1)S(1)}, u32[]{:S(2)}, u32[]{:S(2)}) collective-permute-start(bf16[72,16,64]{2,1,0:T(8,128)(2,1)S(1)} %multiply_convert_fusion), channel_id=1, source_target_pairs={{0,256},{256,0},{4,260},{260,4},{8,264},{264,8},{12,268},{268,12},... | collective-permute-start | bytes 442376 | tf_op jit(solution)/shard_map/ppermute | solution.py:32
  158.5 8.2 %collective-permute-done.3 = bf16[72,16,64]{2,1,0:T(8,128)(2,1)S(1)} collective-permute-done((bf16[72,16,64]{2,1,0:T(8,128)(2,1)S(1)}, bf16[72,16,64]{2,1,0:T(8,128)(2,1)S(1)}, u32[]{:S(2)}, u32[]{:S(2)}) %collective-permute-start.3) | collective-permute-done | bytes 147488 | tf_op jit(solution)/shard_map/ppermute | solution.py:32
  166.8 0.2 pad_maximum_fusion.2
  167.0 10.9 %all_to_all.27 = bf16[72,16,128]{2,1,0:T(8,128)(2,1)S(1)} all-to-all(bf16[72,16,128]{2,1,0:T(8,128)(2,1)S(1)} %pad_maximum_fusion.2), channel_id=1, replica_groups=mesh['elem'=128,'lev'=4] {'lev'}, dimensions={0} | all-to-all | bytes 589824 | tf_op jit(solution)/shard_map/all_to_all | solution.py:188
  177.8 2.9 %copy.82 = f32[4,18,16,128]{1,2,3,0:T(8,128)} copy(bf16[4,18,16,128]{3,2,1,0:T(8,128)(2,1)S(1)} %bitcast.171) | data formatting | bytes 884736 | tf_op jit(solution)/shard_map/convert_element_type | solution.py:189
  180.7 5.6 %bitcast_add_fusion = f32[18,16,512]{0,1,2:T(8,128)} fusion(f32[4,18,16,128]{1,2,3,0:T(8,128)} %copy.82, f32[512,18,16]{1,2,0:T(8,128)} %gather_fusion.3, pred[512]{0:T(512)(128)(4,1)S(1)} %compare_and_fusion), kind=kLoop, calls=%fused_computation.5 | loop fusion | flops 294912 | bytes 1769984 | tf_op jit(solution)/shard_map/add | solution.py:189
  186.3 3.7 %copy.83 = f32[18,16,512]{2,1,0:T(8,128)} copy(f32[18,16,512]{0,1,2:T(8,128)} %bitcast_add_fusion) | data formatting | bytes 1179648 | tf_op jit(solution)/shard_map/add | solution.py:189
  (44 shorter events, 0.8 us)
Async XLA Ops:
  0.0 151.4 %copy-start = (bf16[512,72]{0,1:T(8,128)(2,1)S(1)}, bf16[512,72]{0,1:T(8,128)(2,1)}, u32[]{:S(2)}) copy-start(bf16[512,72]{0,1:T(8,128)(2,1)} %param.24) | copy-start | bytes 221188
  21.6 5.1 %copy-start.6 = (f32[4,4,1,1,1]{1,0,4,3,2:T(4,128)S(1)}, f32[4,4,1,1,1]{1,0,4,3,2:T(4,128)}, u32[]{:S(2)}) copy-start(f32[4,4,1,1,1]{1,0,4,3,2:T(4,128)} %constant.115) | copy-start | bytes 196
  29.0 3.3 %copy-start.3 = (f32[18,4,4,8,64]{4,1,3,2,0:T(4,128)S(1)}, f32[18,4,4,8,64]{4,1,3,2,0:T(4,128)}, u32[]{:S(2)}) copy-start(f32[18,4,4,8,64]{4,1,3,2,0:T(4,128)} %copy.60) | copy-start | bytes 1769476
  34.6 3.8 %copy-start.4 = (bf16[18,16,512]{2,1,0:T(8,128)(2,1)S(1)}, bf16[18,16,512]{2,1,0:T(8,128)(2,1)}, u32[]{:S(2)}) copy-start(bf16[18,16,512]{2,1,0:T(8,128)(2,1)} %param.20) | copy-start | bytes 884740
  45.3 2.9 %copy-start.5 = (bf16[18,16,512]{2,1,0:T(8,128)(2,1)S(1)}, bf16[18,16,512]{2,1,0:T(8,128)(2,1)}, u32[]{:S(2)}) copy-start(bf16[18,16,512]{2,1,0:T(8,128)(2,1)} %param.21) | copy-start | bytes 884740
  67.4 1.0 copy-start.1
  68.4 4.1 %copy-start.7 = (s32[1,512]{1,0:T(1,128)S(1)}, s32[1,512]{1,0:T(1,128)}, u32[]{:S(2)}) copy-start(s32[1,512]{1,0:T(1,128)} %param.22) | copy-start | bytes 6148
  68.4 4.2 %copy-start.8 = (f32[2,512]{1,0:T(2,128)S(1)}, f32[2,512]{1,0:T(2,128)}, u32[]{:S(2)}) copy-start(f32[2,512]{1,0:T(2,128)} %param.27) | copy-start | bytes 12292
  68.5 18.2 %collective-permute-start = (f32[18,4,1,64]{3,2,1,0:T(1,128)S(1)}, f32[18,4,1,64]{3,2,1,0:T(1,128)S(1)}, u32[]{:S(2)}, u32[]{:S(2)}) collective-permute-start(f32[18,4,1,64]{3,2,1,0:T(1,128)S(1)} %slice.162), channel_id=1, source_target_pairs={{0,4},{4,8},{8,12},{12,16},{16,20},{20,24},{24,28},{28,32},{32,36}... | collective-permute-start | bytes 55304 | tf_op jit(solution)/shard_map/ppermute | solution.py:19
  86.8 7.3 %collective-permute-start.1 = (f32[18,4,1,64]{3,2,1,0:T(1,128)S(1)}, f32[18,4,1,64]{3,2,1,0:T(1,128)S(1)}, u32[]{:S(2)}, u32[]{:S(2)}) collective-permute-start(f32[18,4,1,64]{3,2,1,0:T(1,128)S(1)} %get-tuple-element.42), channel_id=1, source_target_pairs={{4,0},{8,4},{12,8},{16,12},{20,16},{24,20},{28,24},{32,28},{36,32}... | collective-permute-start | bytes 55304 | tf_op jit(solution)/shard_map/ppermute | solution.py:20
  94.1 1.3 copy-start.2
  95.4 1.1 slice-start
  121.5 11.0 %all-to-all-start = ((bf16[4,2,18432]{2,1,0:T(2,128)(2,1)}), bf16[4,2,18432]{2,1,0:T(2,128)(2,1)S(1)}, u32[]{:S(2)}, u32[]{:S(2)}) async-start(bf16[4,2,18432]{2,1,0:T(2,128)(2,1)} %reshape.229), calls=%async_computation | async-start | bytes 589824 | tf_op jit(solution)/shard_map/all_to_all | solution.py:175
  139.7 11.7 %copy-start.9 = (bf16[2,512,512]{2,1,0:T(8,128)(2,1)S(1)}, bf16[2,512,512]{2,1,0:T(8,128)(2,1)}, u32[]{:S(2)}) copy-start(bf16[2,512,512]{2,1,0:T(8,128)(2,1)} %param.26) | copy-start | bytes 3145732
  139.7 11.7 %copy-start.11 = (f32[512]{0:T(512)S(1)}, f32[512]{0:T(512)}, u32[]{:S(2)}) copy-start(f32[512]{0:T(512)} %param.25) | copy-start | bytes 6148
  139.8 11.2 %collective-permute-start.2 = (bf16[72,16,64]{2,1,0:T(8,128)(2,1)S(1)}, bf16[72,16,64]{2,1,0:T(8,128)(2,1)S(1)}, u32[]{:S(2)}, u32[]{:S(2)}) collective-permute-start(bf16[72,16,64]{2,1,0:T(8,128)(2,1)S(1)} %broadcast_select_fusion.3), channel_id=1, source_target_pairs={{0,256},{256,0},{4,260},{260,4},{8,264},{264,8},{12,268},{268,12},... | collective-permute-start | bytes 442376 | tf_op jit(solution)/shard_map/ppermute | solution.py:32
  151.4 2.5 %copy-start.10 = (bf16[72,512]{1,0:T(8,128)(2,1)S(1)}, bf16[72,512]{1,0:T(8,128)(2,1)}, u32[]{:S(2)}) copy-start(bf16[72,512]{1,0:T(8,128)(2,1)} %param.28) | copy-start | bytes 221188
  156.6 10.1 %collective-permute-start.3 = (bf16[72,16,64]{2,1,0:T(8,128)(2,1)S(1)}, bf16[72,16,64]{2,1,0:T(8,128)(2,1)S(1)}, u32[]{:S(2)}, u32[]{:S(2)}) collective-permute-start(bf16[72,16,64]{2,1,0:T(8,128)(2,1)S(1)} %multiply_convert_fusion), channel_id=1, source_target_pairs={{0,256},{256,0},{4,260},{260,4},{8,264},{264,8},{12,268},{268,12},... | collective-permute-start | bytes 442376 | tf_op jit(solution)/shard_map/ppermute | solution.py:32
where the time goes:
time: 191 us; the launch traced here: 190 us
  local copies, waits for them, and re-layouts  85.5 us (45%)
  waiting for transfers between devices  36 us (19%)
  other arithmetic  24 us (13%)
  starting transfers between devices  16.9 us (9%)
  matrix products  16.3 us (9%)
  blocking collectives  10.9 us (6%)
    unnamed x29, local copies, waits for them, and re-layouts  23 us
    ppermute x2, waiting for transfers between devices, from_partner(): return lax.ppermute(block, axis, route)  17.3 us
    ppermute x1, waiting for transfers between devices, extended(): before = lax.ppermute(last, axis, up)  13.2 us
    reshape x3, local copies, waits for them, and re-layouts, on_device(): jnp.take(thermal_anomaly, patch_permutation_map, axis=2)  12.9 us
    all_to_all x1, blocking collectives, on_device(): lax.all_to_all(heating, 'lev', split_axis=0, concat_axis=2, tiled=True)  10.9 us
    gather x2, local copies, waits for them, and re-layouts, on_device(): jnp.take(meridional_velocity, patch_permutation_map, axis=2)  7.52 us
    gather x2, local copies, waits for them, and re-layouts, on_device(): jnp.take(zonal_velocity, patch_permutation_map, axis=2).astype(jnp.float32)  6.87 us
    dot_general x2, matrix products, along_first(): jnp.einsum('ik,lkjxy->lijxy', table, field, precision=lax.Precision.HIGHEST)  5.93 us
  transfers between devices with their start and end apart: 5, of which 4 were waited for; matrix products, arithmetic and copies ran while one was open for 3% of the time, Pallas kernels for 0%

commit v1 on v0

v1 whole, which is shorter than its diff:
```python
import functools
import math

import jax
import jax.numpy as jnp
import numpy as np
from jax import lax
from jax.experimental import pallas as pl
from jax.experimental.pallas import tpu as pltpu
from jax.sharding import PartitionSpec as P

MESH = pl.DeviceIdType.MESH
F32 = jnp.float32
BF16 = jnp.bfloat16
LEV = 4
NL = 18
NODES = 16
ROWS = NL * NODES
NE = 512
HALF = ROWS // 2
LEVELS = NL * LEV
UNITS = 512
NT = (((1,), (1,)), ((), ()))


def derivative_table():
    nodes = [-1.0, -1.0 / math.sqrt(5.0), 1.0 / math.sqrt(5.0), 1.0]
    table = np.zeros((4, 4))
    for i in range(4):
        for j in range(4):
            if i == j:
                table[i, j] = sum(1.0 / (nodes[i] - nodes[m]) for m in range(4) if m != i)
            else:
                upper = lower = 1.0
                for m in range(4):
                    if m != i and m != j:
                        upper *= nodes[i] - nodes[m]
                    if m != j:
                        lower *= nodes[j] - nodes[m]
                table[i, j] = upper / lower
    return table


def derivative_blocks():
    table = derivative_table()
    eye4, eye9 = np.eye(4), np.eye(HALF // NODES)
    first = np.kron(table, eye4)
    second = np.kron(eye4, table)
    blocks = [0.05 * first, 0.05 * second, 0.005 * (first @ first + second @ second)]
    return np.concatenate([np.kron(eye9, b) for b in blocks]).astype(np.float32)


def kernel(
    t_hbm, u_hbm, v_hbm, pos_hbm, flag_hbm, d_hbm, w0_hbm, b0_hbm, wi_hbm, bi_hbm, wr_hbm,
    out_hbm,
    t_v, u_v, v_v, pos_v, flag_v, d_v, w0_v, b0_v, wi_v, bi_v, wr_v,
    q_s, tg_s, ag_s, dd_s, fl_s, w0_s, wi_s, bias_s,
    halo_s, halo_out, halo_in, col_s, col_out, col_in, x_s, h_s, heat_out, heat_in, hin_s, sum_s, out_v,
    in_sem, out_sem, halo_send, halo_recv, col_send, col_recv, heat_send, heat_recv,
):
    me = lax.axis_index("lev")
    elem = lax.axis_index("elem")
    count = lax.axis_size("elem")
    nxt = lax.rem(elem + 1, count)
    prv = lax.rem(elem + count - 1, count)
    peers = [lax.rem(me + d, LEV) for d in (2, 1, 3)]

    loads = {}
    pairs = [
        ("pos", pos_hbm, pos_v), ("t", t_hbm, t_v), ("d", d_hbm, d_v), ("u", u_hbm, u_v),
        ("v", v_hbm, v_v), ("flag", flag_hbm, flag_v), ("w0", w0_hbm, w0_v), ("b0", b0_hbm, b0_v),
        ("bi", bi_hbm, bi_v), ("wi", wi_hbm, wi_v), ("wr", wr_hbm, wr_v),
    ]
    for n, (name, src, dst) in enumerate(pairs):
        loads[name] = pltpu.make_async_copy(src, dst, in_sem.at[n])
        loads[name].start()

    barrier = pltpu.get_barrier_semaphore()
    for p in peers:
        pl.semaphore_signal(barrier, inc=1, device_id=(elem, p), device_id_type=MESH)
    for e in (nxt, prv):
        pl.semaphore_signal(barrier, inc=1, device_id=(e, me), device_id_type=MESH)

    loads["pos"].wait()
    slot = lax.rem(pos_v[...] + 64, NE)
    for r in range(0, NE, 128):
        rows = lax.broadcasted_iota(jnp.int32, (128, NE), 0) + r
        q_s[pl.ds(r, 128), :] = jnp.where(rows == slot, 1.0, 0.0).astype(BF16)

    loads["t"].wait()
    loads["flag"].wait()
    flags = jnp.broadcast_to(flag_v[...].astype(F32), (16, NE)).astype(BF16)
    t_b = t_v[...].astype(BF16)
    both = lax.dot_general(
        jnp.concatenate([t_b, flags], axis=0), q_s[...], NT, preferred_element_type=F32
    )
    for c in range(4):
        ag_s[c] = both[:ROWS, 128 * c : 128 * c + 128]
    fl_s[...] = both[ROWS : ROWS + 8]

    loads["d"].wait()
    loads["u"].wait()
    loads["v"].wait()
    deriv = d_v[...].astype(BF16)
    parts = []
    for b in range(2):
        sl = slice(b * HALF, (b + 1) * HALF)
        g = jnp.dot(deriv, t_b[sl], preferred_element_type=F32)
        u = u_v[sl, :].astype(F32)
        v = v_v[sl, :].astype(F32)
        tend = g[2 * HALF :] - u * g[:HALF] - v * g[HALF : 2 * HALF]
        parts.append(tend.astype(BF16))
    tend = lax.dot_general(
        jnp.concatenate(parts, axis=0), q_s[...], NT, preferred_element_type=F32
    )
    for c in range(4):
        tg_s[c] = tend[:, 128 * c : 128 * c + 128]

    lane = lax.broadcasted_iota(jnp.int32, (NL, 128), 1)
    left = lane < 64
    inner = lane % 64

    def node(i, j, c):
        return tg_s[c, pl.ds(4 * i + j, NL, stride=NODES), :]

    halo_s[pl.ds(72, 8), :] = jnp.zeros((8, 128), F32)
    for j in range(4):
        halo_s[pl.ds(j, NL, stride=4), :] = jnp.where(left, node(3, j, 0), node(0, j, 0))
    halo_out[...] = halo_s[...].astype(BF16)
    pl.semaphore_wait(barrier, 5)
    halo_copies = []
    for n, e in enumerate((nxt, prv)):
        copy = pltpu.make_async_remote_copy(
            src_ref=halo_out, dst_ref=halo_in.at[n], send_sem=halo_send.at[n],
            recv_sem=halo_recv.at[n], device_id=(e, me), device_id_type=MESH,
        )
        copy.start()
        halo_copies.append(copy)

    def dss(c, halo):
        t = {(i, j): node(i, j, c) for i in range(4) for j in range(4)}
        for j in range(4):
            own0, own3 = t[0, j], t[3, j]
            near0, near3 = own0, own3
            if halo is not None:
                near3, near0 = halo[0][j], halo[1][j]
            after = pltpu.roll(jnp.where(left, node(0, j, (c + 1) % 4), near0), 64, 1)
            before = pltpu.roll(jnp.where(left, near3, node(3, j, (c + 3) % 4)), 64, 1)
            t[3, j] = (own3 + after) * 0.5
            t[0, j] = (own0 + before) * 0.5
        for i in range(4):
            own0, own3 = t[i, 0], t[i, 3]
            after = jnp.where(inner == 63, pltpu.roll(own0, 63, 1), pltpu.roll(own0, 127, 1))
            before = jnp.where(inner == 0, pltpu.roll(own3, 65, 1), pltpu.roll(own3, 1, 1))
            t[i, 3] = (own3 + after) * 0.5
            t[i, 0] = (own0 + before) * 0.5
        for i in range(4):
            for j in range(4):
                p = 4 * i + j
                dd_s[p, :NL, pl.ds(128 * c, 128)] = t[i, j]
                temp = ag_s[c, pl.ds(p, NL, stride=NODES), :]
                col_s[pl.ds(HALF * i + 72 * (c % 2) + j, NL, stride=4), :] = temp + t[i, j]

    col_copies = []

    def send_columns(s):
        col_out[s] = col_s[...].astype(BF16).reshape(LEV, HALF, 128)
        copies = []
        for n, p in enumerate(peers):
            copy = pltpu.make_async_remote_copy(
                src_ref=col_out.at[s, p], dst_ref=col_in.at[s, me], send_sem=col_send.at[s, n],
                recv_sem=col_recv.at[s, n], device_id=(elem, p), device_id_type=MESH,
            )
            copy.start()
            copies.append(copy)
        col_in[s, me] = col_out[s, me]
        col_copies.append(copies)

    dss(2, None)
    dss(3, None)
    send_columns(0)

    for copy in halo_copies:
        copy.wait_recv()
    from_before, from_after = [], []
    for n, store in enumerate((from_before, from_after)):
        halo_s[...] = halo_in[n].astype(F32)
        for j in range(4):
            store.append(halo_s[pl.ds(j, NL, stride=4), :])
    dss(0, (from_before, from_after))
    dss(1, None)
    send_columns(1)

    loads["w0"].wait()
    loads["b0"].wait()
    bias = b0_v[...] * 0.5
    coarse = bias.astype(BF16).astype(F32)
    row8 = lax.broadcasted_iota(jnp.int32, (8, UNITS), 0)
    tail = jnp.where(row8 == 0, coarse, jnp.where(row8 == 1, bias - coarse, 0.0))
    w0 = jnp.concatenate(
        [w0_v[...].astype(F32) * 0.5, tail, jnp.zeros((128 - LEVELS - 8, UNITS), F32)], axis=0
    )
    w0_s[...] = w0.T.astype(BF16)
    loads["bi"].wait()
    for m in range(2):
        bias_s[m] = jnp.broadcast_to(bi_v[pl.ds(m, 1), :] * 0.5, (128, UNITS)).T
    loads["wi"].wait()
    wi_s[...] = wi_v[...] * jnp.asarray(0.5, BF16)
    loads["wr"].wait()

    row8 = lax.broadcasted_iota(jnp.int32, (8, 256), 0)
    ones = jnp.where(row8 < 2, 1.0, 0.0)

    def gate(h):
        return (h + h * jnp.tanh(h)).astype(BF16)

    heat_copies = []
    for s in range(2):
        for copy in col_copies[s]:
            copy.wait_recv()
        for src in range(LEV):
            block = col_in[s, src].astype(F32)
            for h in range(2):
                x_s[pl.ds(288 * h + 72 * src, 72), :] = block[72 * h : 72 * h + 72]

        def step(j, carry):
            x = jnp.concatenate([x_s[pl.ds(288 * h + j, LEVELS, stride=4), :] for h in range(2)], axis=1)
            x = jnp.concatenate([x, ones], axis=0).astype(BF16)
            hid = gate(jnp.dot(w0_s[:, : LEVELS + 8], x, preferred_element_type=F32))
            for m in range(2):
                pre = jnp.dot(wi_s[pl.ds(m * UNITS, UNITS), :], hid, preferred_element_type=F32)
                off = bias_s[m]
                hid = gate(pre + jnp.concatenate([off, off], axis=1))
            heat = jnp.dot(wr_v[...], hid, preferred_element_type=F32)
            for h in range(2):
                h_s[pl.ds(288 * h + j, LEVELS, stride=4), :] = heat[:, 128 * h : 128 * h + 128]
            return carry

        lax.fori_loop(0, 4, step, 0)
        for dst in range(LEV):
            block = jnp.concatenate([h_s[pl.ds(288 * h + 72 * dst, 72), :] for h in range(2)], axis=0)
            heat_out[s, dst] = block.astype(BF16)
        copies = []
        for n, p in enumerate(peers):
            copy = pltpu.make_async_remote_copy(
                src_ref=heat_out.at[s, p], dst_ref=heat_in.at[s, me], send_sem=heat_send.at[s, n],
                recv_sem=heat_recv.at[s, n], device_id=(elem, p), device_id_type=MESH,
            )
            copy.start()
            copies.append(copy)
        heat_in[s, me] = heat_out[s, me]
        heat_copies.append(copies)

    for s in range(2):
        for copy in heat_copies[s]:
            copy.wait_recv()
        for q in range(LEV):
            hin_s[...] = heat_in[s, q].astype(F32)
            for h in range(2):
                c = 2 * (1 - s) + h
                lanes = pl.ds(128 * c, 128)
                day = fl_s[pl.ds(0, 1), lanes]
                for j in range(4):
                    p = 4 * q + j
                    heat = hin_s[pl.ds(72 * h + j, NL, stride=4), :]
                    sum_s[h, pl.ds(p, NL, stride=NODES), :] = dd_s[p, :NL, lanes] + heat * day
        lanes = pl.ds(256 * (1 - s), 256)
        total = jnp.concatenate([sum_s[0], sum_s[1]], axis=1).astype(BF16)
        back = jnp.dot(total, q_s[lanes, :], preferred_element_type=F32)
        if s == 0:
            out_v[...] = t_v[...] + back
        else:
            out_v[...] = out_v[...] + back
    store = pltpu.make_async_copy(out_v, out_hbm, out_sem)
    store.start()

    for copy in halo_copies:
        copy.wait_send()
    for copies in col_copies + heat_copies:
        for copy in copies:
            copy.wait_send()
    store.wait()


def on_device(t, u, v, pos, sunlit, w0, b0, wi, bi, wr):
    shape = t.shape
    args = [
        t.reshape(ROWS, NE), u.reshape(ROWS, NE), v.reshape(ROWS, NE), pos, sunlit.reshape(1, NE),
        jnp.asarray(derivative_blocks()), w0.T, b0.reshape(1, UNITS), wi.reshape(2 * UNITS, UNITS),
        bi, wr,
    ]
    vmem = [pltpu.VMEM(a.shape, a.dtype) for a in args]
    dma = pltpu.SemaphoreType.DMA
    scratch = vmem + [
        pltpu.VMEM((NE, NE), BF16),
        pltpu.VMEM((4, ROWS, 128), F32),
        pltpu.VMEM((4, ROWS, 128), F32),
        pltpu.VMEM((NODES, 24, NE), F32),
        pltpu.VMEM((8, NE), F32),
        pltpu.VMEM((UNITS, 128), BF16),
        pltpu.VMEM((2 * UNITS, UNITS), BF16),
        pltpu.VMEM((2, UNITS, 128), F32),
        pltpu.VMEM((80, 128), F32),
        pltpu.VMEM((80, 128), BF16),
        pltpu.VMEM((2, 80, 128), BF16),
        pltpu.VMEM((LEV * HALF, 128), F32),
        pltpu.VMEM((2, LEV, HALF, 128), BF16),
        pltpu.VMEM((2, LEV, HALF, 128), BF16),
        pltpu.VMEM((LEV * HALF, 128), F32),
        pltpu.VMEM((LEV * HALF, 128), F32),
        pltpu.VMEM((2, LEV, HALF, 128), BF16),
        pltpu.VMEM((2, LEV, HALF, 128), BF16),
        pltpu.VMEM((HALF, 128), F32),
        pltpu.VMEM((2, ROWS, 128), F32),
        pltpu.VMEM((ROWS, NE), F32),
        dma((len(args),)), dma, dma((2,)), dma((2,)), dma((2, 3)), dma((2, 3)), dma((2, 3)), dma((2, 3)),
    ]
    any_spec = pl.BlockSpec(memory_space=pl.ANY)
    out = pl.pallas_call(
        kernel,
        out_shape=jax.ShapeDtypeStruct((ROWS, NE), F32),
        in_specs=[any_spec] * len(args),
        out_specs=any_spec,
        scratch_shapes=scratch,
        compiler_params=pltpu.CompilerParams(
            collective_id=0, has_side_effects=True, vmem_limit_bytes=60 * 2**20
        ),
        name="section",
    )(*args)
    return out.reshape(shape)


def solution(mesh):
    in_specs = (
        P("lev", None, "elem"), P("lev", None, "elem"), P("lev", None, "elem"), P("elem", None),
        P("elem"), P(), P(), P(), P(), P(),
    )
    out_specs = P("lev", None, "elem")
    return jax.shard_map(
        on_device, mesh=mesh, in_specs=in_specs, out_specs=out_specs, check_vma=False
    )
```

time: 191 us -> 36.1 us (0.19)
  local copies, waits for them, and re-layouts: 85.5 us -> 1.93 us
  waiting for transfers between devices: 36 us -> 0 us
  Pallas kernels: 0 us -> 33.9 us
  other arithmetic: 24 us -> 0 us
  starting transfers between devices: 16.9 us -> 0 us
  matrix products: 16.3 us -> 0 us
  blocking collectives: 10.9 us -> 0 us
    pallas_call x0 -> x1, Pallas kernels: none -> 33.9 us  [on_device(): pl.pallas_call(kernel, out_shape=jax.ShapeDtypeStruct((ROWS, NE), F32), i...]
    ppermute x4 -> x0, waiting for transfers between devices: 30.5 us -> none  [the longest x2 17.3 us: from_partner(): return lax.ppermute(block, axis, route)]
    gather x6 -> x0, local copies, waits for them, and re-layouts: 24.7 us -> none  [the longest x2 7.52 us: on_device(): jnp.take(meridional_velocity, patch_permutation_map, axis=2)]
    reshape x8 -> x0, local copies, waits for them, and re-layouts: 21.8 us -> none  [the longest x3 12.9 us: on_device(): jnp.take(thermal_anomaly, patch_permutation_map, axis=2)]
    unnamed x29 -> x1, local copies, waits for them, and re-layouts: 23 us -> 1.93 us
    dot_general x6 -> x0, matrix products: 16.3 us -> none  [the longest x2 5.93 us: along_first(): jnp.einsum('ik,lkjxy->lijxy', table, field, precision=lax.Precision.HIGHEST)]
    ppermute x4 -> x0, starting transfers between devices: 11.4 us -> none  [the longest x1 4.04 us: extended(): before = lax.ppermute(last, axis, up)]
    all_to_all x1 -> x0, blocking collectives: 10.9 us -> none  [on_device(): lax.all_to_all(heating, 'lev', split_axis=0, concat_axis=2, tiled=True)]
  transfers between devices with their start and end apart: 5 -> 0, of which waited for: 4 -> 0; matrix products, arithmetic and copies ran while one was open for 3% -> 0% of each run, Pallas kernels for 0% -> 0%
where the time goes in v1:
time: 36.1 us; the launch traced here: 35.9 us
  Pallas kernels  33.9 us (94%)
  local copies, waits for them, and re-layouts  1.93 us (5%)
    pallas_call x1, Pallas kernels, on_device(): pl.pallas_call(kernel, out_shape=jax.ShapeDtypeStruct((ROWS, NE), F32), i...  33.9 us
    unnamed x1, local copies, waits for them, and re-layouts  1.93 us

profile of v1, /device:TPU:1, one launch (start us, length us, event | category | flops | bytes accessed | tf_op | source)
XLA Modules:
  0.0 35.9 jit_solution(1074518822838443527)
XLA Ops:
  0.0 33.9 %section.1 = f32[288,512]{1,0:T(8,128)} custom-call(f32[288,512]{1,0:T(8,128)} %bitcast.10, bf16[288,512]{1,0:T(8,128)(2,1)} %bitcast.11, bf16[288,512]{1,0:T(8,128)(2,1)} %bitcast.12, s32[1,512]{1,0:T(1,128)} %pos_hbm.1, s32[1,512]{1,0:T(1,128)} %bitcast.14, f32[432,144]{1,0:T(8,128)} %constant.2.clone.d_hbm, bf16[72,512]{1,0:T(8,128)(2,1)} %bitcast.13, ...), custom_call_target="tpu_custom_call" | custom-call | tf_op jit(solution)/shard_map/section/pallas_call | solution.py:319
  33.9 1.9 %copy.13 = f32[18,16,512]{2,1,0:T(8,128)} copy(f32[18,16,512]{2,1,0:T(8,128)} %bitcast.8) | data formatting | bytes 1179648

commit v2 on v1

--- a/solution.py
+++ b/solution.py
@@ -52,11 +52,11 @@
 
 def kernel(
     t_hbm, u_hbm, v_hbm, pos_hbm, flag_hbm, d_hbm, w0_hbm, b0_hbm, wi_hbm, bi_hbm, wr_hbm,
-    out_hbm,
+    out_v,
     t_v, u_v, v_v, pos_v, flag_v, d_v, w0_v, b0_v, wi_v, bi_v, wr_v,
     q_s, tg_s, ag_s, dd_s, fl_s, w0_s, wi_s, bias_s,
-    halo_s, halo_out, halo_in, col_s, col_out, col_in, x_s, h_s, heat_out, heat_in, hin_s, sum_s, out_v,
-    in_sem, out_sem, halo_send, halo_recv, col_send, col_recv, heat_send, heat_recv,
+    halo_s, halo_out, halo_in, col_s, col_out, col_in, x_s, h_s, heat_out, heat_in, hin_s, sum_s,
+    in_sem, halo_send, halo_recv, col_send, col_recv, heat_send, heat_recv,
 ):
     me = lax.axis_index("lev")
     elem = lax.axis_index("elem")
@@ -81,14 +81,14 @@
     for e in (nxt, prv):
         pl.semaphore_signal(barrier, inc=1, device_id=(e, me), device_id_type=MESH)
 
-    loads["pos"].wait()
+    loads.pop("pos").wait()
     slot = lax.rem(pos_v[...] + 64, NE)
     for r in range(0, NE, 128):
         rows = lax.broadcasted_iota(jnp.int32, (128, NE), 0) + r
         q_s[pl.ds(r, 128), :] = jnp.where(rows == slot, 1.0, 0.0).astype(BF16)
 
-    loads["t"].wait()
-    loads["flag"].wait()
+    loads.pop("t").wait()
+    loads.pop("flag").wait()
     flags = jnp.broadcast_to(flag_v[...].astype(F32), (16, NE)).astype(BF16)
     t_b = t_v[...].astype(BF16)
     both = lax.dot_general(
@@ -98,9 +98,9 @@
         ag_s[c] = both[:ROWS, 128 * c : 128 * c + 128]
     fl_s[...] = both[ROWS : ROWS + 8]
 
-    loads["d"].wait()
-    loads["u"].wait()
-    loads["v"].wait()
+    loads.pop("d").wait()
+    loads.pop("u").wait()
+    loads.pop("v").wait()
     deriv = d_v[...].astype(BF16)
     parts = []
     for b in range(2):
@@ -191,8 +191,8 @@
     dss(1, None)
     send_columns(1)
 
-    loads["w0"].wait()
-    loads["b0"].wait()
+    loads.pop("w0").wait()
+    loads.pop("b0").wait()
     bias = b0_v[...] * 0.5
     coarse = bias.astype(BF16).astype(F32)
     row8 = lax.broadcasted_iota(jnp.int32, (8, UNITS), 0)
@@ -201,14 +201,14 @@
         [w0_v[...].astype(F32) * 0.5, tail, jnp.zeros((128 - LEVELS - 8, UNITS), F32)], axis=0
     )
     w0_s[...] = w0.T.astype(BF16)
-    loads["bi"].wait()
+    loads.pop("bi").wait()
     for m in range(2):
         bias_s[m] = jnp.broadcast_to(bi_v[pl.ds(m, 1), :] * 0.5, (128, UNITS)).T
-    loads["wi"].wait()
+    loads.pop("wi").wait()
     wi_s[...] = wi_v[...] * jnp.asarray(0.5, BF16)
-    loads["wr"].wait()
-
-    row8 = lax.broadcasted_iota(jnp.int32, (8, 256), 0)
+    loads.pop("wr").wait()
+
+    row8 = lax.broadcasted_iota(jnp.int32, (8, 1024), 0)
     ones = jnp.where(row8 < 2, 1.0, 0.0)
 
     def gate(h):
@@ -223,20 +223,19 @@
             for h in range(2):
                 x_s[pl.ds(288 * h + 72 * src, 72), :] = block[72 * h : 72 * h + 72]
 
-        def step(j, carry):
-            x = jnp.concatenate([x_s[pl.ds(288 * h + j, LEVELS, stride=4), :] for h in range(2)], axis=1)
-            x = jnp.concatenate([x, ones], axis=0).astype(BF16)
-            hid = gate(jnp.dot(w0_s[:, : LEVELS + 8], x, preferred_element_type=F32))
-            for m in range(2):
-                pre = jnp.dot(wi_s[pl.ds(m * UNITS, UNITS), :], hid, preferred_element_type=F32)
-                off = bias_s[m]
-                hid = gate(pre + jnp.concatenate([off, off], axis=1))
-            heat = jnp.dot(wr_v[...], hid, preferred_element_type=F32)
-            for h in range(2):
-                h_s[pl.ds(288 * h + j, LEVELS, stride=4), :] = heat[:, 128 * h : 128 * h + 128]
-            return carry
-
-        lax.fori_loop(0, 4, step, 0)
+        x = jnp.concatenate(
+            [x_s[pl.ds(288 * h + j, LEVELS, stride=4), :] for j in range(4) for h in range(2)], axis=1
+        )
+        x = jnp.concatenate([x, ones], axis=0).astype(BF16)
+        hid = gate(jnp.dot(w0_s[:, : LEVELS + 8], x, preferred_element_type=F32))
+        for m in range(2):
+            pre = jnp.dot(wi_s[pl.ds(m * UNITS, UNITS), :], hid, preferred_element_type=F32)
+            off = bias_s[m]
+            hid = gate(pre + jnp.concatenate([off] * 8, axis=1))
+        heat = jnp.dot(wr_v[...], hid, preferred_element_type=F32)
+        for n in range(8):
+            j, h = divmod(n, 2)
+            h_s[pl.ds(288 * h + j, LEVELS, stride=4), :] = heat[:, 128 * n : 128 * n + 128]
         for dst in range(LEV):
             block = jnp.concatenate([h_s[pl.ds(288 * h + 72 * dst, 72), :] for h in range(2)], axis=0)
             heat_out[s, dst] = block.astype(BF16)
@@ -271,15 +270,12 @@
             out_v[...] = t_v[...] + back
         else:
             out_v[...] = out_v[...] + back
-    store = pltpu.make_async_copy(out_v, out_hbm, out_sem)
-    store.start()
 
     for copy in halo_copies:
         copy.wait_send()
     for copies in col_copies + heat_copies:
         for copy in copies:
             copy.wait_send()
-    store.wait()
 
 
 def on_device(t, u, v, pos, sunlit, w0, b0, wi, bi, wr):
@@ -312,15 +308,14 @@
         pltpu.VMEM((2, LEV, HALF, 128), BF16),
         pltpu.VMEM((HALF, 128), F32),
         pltpu.VMEM((2, ROWS, 128), F32),
-        pltpu.VMEM((ROWS, NE), F32),
-        dma((len(args),)), dma, dma((2,)), dma((2,)), dma((2, 3)), dma((2, 3)), dma((2, 3)), dma((2, 3)),
+        dma((len(args),)), dma((2,)), dma((2,)), dma((2, 3)), dma((2, 3)), dma((2, 3)), dma((2, 3)),
     ]
-    any_spec = pl.BlockSpec(memory_space=pl.ANY)
+    any_spec = pl.BlockSpec(memory_space=pltpu.HBM)
     out = pl.pallas_call(
         kernel,
-        out_shape=jax.ShapeDtypeStruct((ROWS, NE), F32),
+        out_shape=pltpu.VMEM((ROWS, NE), F32),
         in_specs=[any_spec] * len(args),
-        out_specs=any_spec,
+        out_specs=pl.BlockSpec(memory_space=pltpu.VMEM),
         scratch_shapes=scratch,
         compiler_params=pltpu.CompilerParams(
             collective_id=0, has_side_effects=True, vmem_limit_bytes=60 * 2**20

time: 36.1 us -> 30.4 us (0.84)
  Pallas kernels: 33.9 us -> 29.4 us
  local copies, waits for them, and re-layouts: 1.93 us -> 0.82 us
    pallas_call x1, Pallas kernels: 33.9 us -> 29.4 us  [on_device(): pl.pallas_call(kernel, out_shape=pltpu.VMEM((ROWS, NE), F32), in_specs=[a...]
    unnamed x1, local copies, waits for them, and re-layouts: 1.93 us -> 0.82 us
where the time goes in v2:
time: 30.4 us; the launch traced here: 30.3 us
  Pallas kernels  29.4 us (97%)
  local copies, waits for them, and re-layouts  0.82 us (3%)
    pallas_call x1, Pallas kernels, on_device(): pl.pallas_call(kernel, out_shape=pltpu.VMEM((ROWS, NE), F32), in_specs=[a...  29.4 us
    unnamed x1, local copies, waits for them, and re-layouts  0.82 us

profile of v2, /device:TPU:1, one launch (start us, length us, event | category | flops | bytes accessed | tf_op | source)
XLA Modules:
  0.0 30.3 jit_solution(9219182286722926734)
XLA Ops:
  0.0 29.4 %section.1 = f32[288,512]{1,0:T(8,128)S(1)} custom-call(f32[288,512]{1,0:T(8,128)} %bitcast.10, bf16[288,512]{1,0:T(8,128)(2,1)} %bitcast.11, bf16[288,512]{1,0:T(8,128)(2,1)} %bitcast.12, s32[1,512]{1,0:T(1,128)} %pos_hbm.1, s32[1,512]{1,0:T(1,128)} %bitcast.14, f32[432,144]{1,0:T(8,128)} %constant.2.clone.d_hbm, bf16[72,512]{1,0:T(8,128)(2,1)} %bitcast.13, ...), custom_call_target="tpu_custom_call" | custom-call | tf_op jit(solution)/shard_map/section/pallas_call | solution.py:314
  29.5 0.8 %copy.13 = f32[18,16,512]{2,1,0:T(8,128)} copy(f32[18,16,512]{2,1,0:T(8,128)S(1)} %bitcast.8) | data formatting | bytes 1179648

commit v3 on v2

v3 whole, which is shorter than its diff:
```python
import functools
import math

import jax
import jax.numpy as jnp
import numpy as np
from jax import lax
from jax.experimental import pallas as pl
from jax.experimental.pallas import tpu as pltpu
from jax.sharding import PartitionSpec as P

MESH = pl.DeviceIdType.MESH
F32 = jnp.float32
BF16 = jnp.bfloat16
LEV = 4
NL = 18
NODES = 16
ROWS = NL * NODES
NE = 512
BLOCK = 48
CHUNKS = (2, 3, 1, 0)
TALL = 80
SMALL = 32
LEVELS = NL * LEV
UNITS = 512
NT = (((1,), (1,)), ((), ()))


def derivative_table():
    nodes = [-1.0, -1.0 / math.sqrt(5.0), 1.0 / math.sqrt(5.0), 1.0]
    table = np.zeros((4, 4))
    for i in range(4):
        for j in range(4):
            if i == j:
                table[i, j] = sum(1.0 / (nodes[i] - nodes[m]) for m in range(4) if m != i)
            else:
                upper = lower = 1.0
                for m in range(4):
                    if m != i and m != j:
                        upper *= nodes[i] - nodes[m]
                    if m != j:
                        lower *= nodes[j] - nodes[m]
                table[i, j] = upper / lower
    return table


def derivative_blocks():
    table = derivative_table()
    eye4, eye_block = np.eye(4), np.eye(BLOCK // NODES)
    first = np.kron(table, eye4)
    second = np.kron(eye4, table)
    blocks = [0.05 * first, 0.05 * second, 0.005 * (first @ first + second @ second)]
    return np.concatenate([np.kron(eye_block, b) for b in blocks]).astype(np.float32)


def kernel(
    t_hbm, u_hbm, v_hbm, pos_hbm, flag_hbm, d_hbm, w0_hbm, b0_hbm, wi_hbm, bi_hbm, wr_hbm,
    out_v,
    t_v, u_v, v_v, pos_v, flag_v, d_v, w0_v, b0_v, wi_v, bi_v, wr_v,
    q_s, tg_s, ag_s, dd_s, fl_s, w0_s, wi_s, bias_s,
    small_s, halo_out, halo_in, pre_out, pre_in, late_out, late_in, col_s, x_s, h_s, hin_s, sum_s,
    col_out, col_in, heat_out, heat_in,
    in_sem, ready, halo_send, halo_recv, col_send, col_recv, heat_send, heat_recv,
    pre_send, pre_recv, late_send, late_recv,
):
    me = lax.axis_index("lev")
    elem = lax.axis_index("elem")
    count = lax.axis_size("elem")
    nxt = lax.rem(elem + 1, count)
    prv = lax.rem(elem + count - 1, count)
    peers = [lax.rem(me + d, LEV) for d in (2, 1, 3)]

    loads = {}
    pairs = [
        ("pos", pos_hbm, pos_v), ("t", t_hbm, t_v), ("d", d_hbm, d_v), ("u", u_hbm, u_v),
        ("v", v_hbm, v_v), ("flag", flag_hbm, flag_v), ("w0", w0_hbm, w0_v), ("b0", b0_hbm, b0_v),
        ("bi", bi_hbm, bi_v), ("wi", wi_hbm, wi_v), ("wr", wr_hbm, wr_v),
    ]
    for n, (name, src, dst) in enumerate(pairs):
        loads[name] = pltpu.make_async_copy(src, dst, in_sem.at[n])
        loads[name].start()

    barrier = pltpu.get_barrier_semaphore()
    for p in peers:
        pl.semaphore_signal(barrier, inc=1, device_id=(elem, p), device_id_type=MESH)
    for q in range(LEV):
        pl.semaphore_signal(barrier, inc=1, device_id=(prv, q), device_id_type=MESH)

    loads.pop("pos").wait()
    slot = lax.rem(pos_v[...] + 64, NE)
    for r in range(0, NE, 128):
        rows = lax.broadcasted_iota(jnp.int32, (128, NE), 0) + r
        q_s[pl.ds(r, 128), :] = jnp.where(rows == slot, 1.0, 0.0).astype(BF16)

    loads.pop("d").wait()
    deriv = d_v[...].astype(BF16)
    loads.pop("t").wait()
    t_hi = t_v[...].astype(BF16)
    loads.pop("u").wait()
    loads.pop("v").wait()
    parts = []
    for b in range(0, ROWS, BLOCK):
        sl = slice(b, b + BLOCK)
        g = jnp.dot(deriv, t_hi[sl], preferred_element_type=F32)
        u = u_v[sl, :].astype(F32)
        v = v_v[sl, :].astype(F32)
        tend = g[2 * BLOCK :] - u * g[:BLOCK] - v * g[BLOCK : 2 * BLOCK]
        parts.append(tend.astype(BF16))
    tend = jnp.concatenate(parts, axis=0)
    tg_s[0] = lax.dot_general(tend, q_s[:128, :], NT, preferred_element_type=F32)

    lane = lax.broadcasted_iota(jnp.int32, (NL, 128), 1)
    left = lane < 64
    inner = lane % 64

    def node(i, j, c):
        return tg_s[c, pl.ds(4 * i + j, NL, stride=NODES), :]

    def along_second(t, i):
        own0, own3 = t[i, 0], t[i, 3]
        after = jnp.where(inner == 63, pltpu.roll(own0, 63, 1), pltpu.roll(own0, 127, 1))
        before = jnp.where(inner == 0, pltpu.roll(own3, 65, 1), pltpu.roll(own3, 1, 1))
        t[i, 3] = (own3 + after) * 0.5
        t[i, 0] = (own0 + before) * 0.5

    edge = {(i, j): node(i, j, 0) for i in (0, 3) for j in range(4)}
    along_second(edge, 0)
    along_second(edge, 3)
    small_s[...] = jnp.zeros(small_s.shape, F32)
    for j in range(4):
        small_s[pl.ds(SMALL * j, NL), :] = jnp.where(left, edge[3, j], edge[0, j])
    halo_out[...] = small_s[...].astype(BF16).reshape(LEV, SMALL, 128)
    pl.semaphore_wait(barrier, 7)
    targets = [lax.rem(me + d, LEV) for d in range(LEV)]
    halo_copies = [
        [
            pltpu.make_async_remote_copy(
                src_ref=halo_out.at[q], dst_ref=halo_in.at[n, me], send_sem=halo_send.at[n, d],
                recv_sem=halo_recv.at[n, d], device_id=(e, q), device_id_type=MESH,
            )
            for d, q in enumerate(targets)
        ]
        for n, e in enumerate((nxt, prv))
    ]
    for copy in halo_copies[0]:
        copy.start()
    for q in targets:
        pl.semaphore_signal(ready, inc=1, device_id=(nxt, q), device_id_type=MESH)

    def send_back():
        pl.semaphore_wait(ready, LEV)
        for copy in halo_copies[1]:
            copy.start()

    rest = lax.dot_general(tend, q_s[128:, :], NT, preferred_element_type=F32)
    for c in range(1, 4):
        tg_s[c] = rest[:, 128 * (c - 1) : 128 * c]
    loads.pop("flag").wait()
    flags = jnp.broadcast_to(flag_v[...].astype(F32), (16, NE)).astype(BF16)
    t_lo = (t_v[...] - t_hi.astype(F32)).astype(BF16)
    both = lax.dot_general(
        jnp.concatenate([t_hi, t_lo, flags], axis=0), q_s[...], NT, preferred_element_type=F32
    )
    for c in range(4):
        lanes = slice(128 * c, 128 * c + 128)
        ag_s[c] = both[:ROWS, lanes] + both[ROWS : 2 * ROWS, lanes]
    fl_s[...] = both[2 * ROWS : 2 * ROWS + 8]

    def dss(part):
        c = CHUNKS[part]
        t = {(i, j): node(i, j, c) for i in range(4) for j in range(4)}
        for j in range(4):
            own0, own3 = t[0, j], t[3, j]
            near0, near3 = own0, own3
            if c == 0:
                near0 = near3 = jnp.zeros((NL, 128), F32)
            after = pltpu.roll(jnp.where(left, node(0, j, (c + 1) % 4), near0), 64, 1)
            before = pltpu.roll(jnp.where(left, near3, node(3, j, (c + 3) % 4)), 64, 1)
            t[3, j] = (own3 + after) * 0.5
            t[0, j] = (own0 + before) * 0.5
        for i in range(4):
            along_second(t, i)
        col = {}
        for i in range(4):
            for j in range(4):
                p = 4 * i + j
                dd_s[c, p, :NL, :] = t[i, j]
                col[i, j] = ag_s[c, pl.ds(p, NL, stride=NODES), :] + t[i, j]
                col_s[pl.ds(TALL * i + j, NL, stride=4), :] = col[i, j]
        return col

    def exchange(out, into, send, recv):
        copies = []
        for n, p in enumerate(peers):
            copy = pltpu.make_async_remote_copy(
                src_ref=out.at[p], dst_ref=into.at[me], send_sem=send.at[n],
                recv_sem=recv.at[n], device_id=(elem, p), device_id_type=MESH,
            )
            copy.start()
            copies.append(copy)
        into[me] = out[me]
        return copies

    def send_columns(part):
        for i in range(LEV):
            col_s[pl.ds(TALL * i + 72, 8), :] = jnp.zeros((8, 128), F32)
        col_out[part] = col_s[...].astype(BF16).reshape(LEV, TALL, 128)
        return exchange(
            col_out.at[part], col_in.at[part], col_send.at[part], col_recv.at[part]
        )

    def gate(h):
        return (h + h * jnp.tanh(h)).astype(BF16)

    def layers(x):
        width = x.shape[1]
        row8 = lax.broadcasted_iota(jnp.int32, (8, width), 0)
        x = jnp.concatenate([x, jnp.where(row8 < 2, 1.0, 0.0)], axis=0).astype(BF16)
        hid = gate(jnp.dot(w0_s[:, : LEVELS + 8], x, preferred_element_type=F32))
        for m in range(2):
            pre = jnp.dot(wi_s[pl.ds(m * UNITS, UNITS), :], hid, preferred_element_type=F32)
            hid = gate(pre + jnp.concatenate([bias_s[m]] * (width // 128), axis=1))
        return jnp.dot(wr_v[...], hid, preferred_element_type=F32)

    def network(part, copies):
        for copy in copies:
            copy.wait_recv()
        for src in range(LEV):
            x_s[pl.ds(72 * src, 72), :] = col_in[part, src].astype(F32)[:72]
        x = jnp.concatenate([x_s[pl.ds(j, LEVELS, stride=4), :] for j in range(4)], axis=1)
        heat = layers(x)
        for j in range(4):
            h_s[pl.ds(j, LEVELS, stride=4), :] = heat[:, 128 * j : 128 * j + 128]
        pad = jnp.zeros((8, 128), F32)
        for dst in range(LEV):
            block = jnp.concatenate([h_s[pl.ds(72 * dst, 72), :], pad], axis=0)
            heat_out[part, dst] = block.astype(BF16)
        return exchange(
            heat_out.at[part], heat_in.at[part], heat_send.at[part], heat_recv.at[part]
        )

    def unpack(part, late):
        c = CHUNKS[part]
        day = fl_s[pl.ds(0, 1), pl.ds(128 * c, 128)]
        for q in range(LEV):
            hin_s[...] = heat_in[part, q].astype(F32)
            for j in range(4):
                p = 4 * q + j
                heat = hin_s[pl.ds(j, NL, stride=4), :] * day
                if late is not None and q == 0:
                    heat = jnp.where(left, heat, late[j])
                if late is not None and q == 3:
                    heat = jnp.where(left, late[j], heat)
                sum_s[c, pl.ds(p, NL, stride=NODES), :] = dd_s[c, p, :NL, :] + heat

    def accumulate(first, last, base):
        total = jnp.concatenate([sum_s[c] for c in range(first, last)], axis=1).astype(BF16)
        rows = q_s[128 * first : 128 * last, :]
        out_v[...] = base[...] + jnp.dot(total, rows, preferred_element_type=F32)

    col_copies = []
    for part in range(4):
        col = dss(part)
        col_copies.append(send_columns(part))
    for j in range(4):
        small_s[pl.ds(SMALL * j, NL), :] = jnp.where(left, col[3, j], col[0, j])
    pre_out[...] = small_s[...].astype(BF16).reshape(LEV, SMALL, 128)
    pre_copies = exchange(pre_out, pre_in, pre_send, pre_recv)
    closing = lax.rem(elem, count // 2) == 0
    pl.when(jnp.logical_not(closing))(send_back)

    loads.pop("w0").wait()
    loads.pop("b0").wait()
    bias = b0_v[...] * 0.5
    coarse = bias.astype(BF16).astype(F32)
    row8 = lax.broadcasted_iota(jnp.int32, (8, UNITS), 0)
    tail = jnp.where(row8 == 0, coarse, jnp.where(row8 == 1, bias - coarse, 0.0))
    w0 = jnp.concatenate(
        [w0_v[...].astype(F32) * 0.5, tail, jnp.zeros((128 - LEVELS - 8, UNITS), F32)], axis=0
    )
    w0_s[...] = w0.T.astype(BF16)
    loads.pop("bi").wait()
    for m in range(2):
        bias_s[m] = jnp.broadcast_to(bi_v[pl.ds(m, 1), :] * 0.5, (128, UNITS)).T
    loads.pop("wi").wait()
    wi_s[...] = wi_v[...] * jnp.asarray(0.5, BF16)
    loads.pop("wr").wait()

    heat_copies = [network(part, col_copies[part]) for part in range(4)]
    pl.when(closing)(send_back)
    for copy in halo_copies[0] + halo_copies[1] + pre_copies:
        copy.wait_recv()
    added = []
    for src in range(LEV):
        edges = jnp.where(left, halo_in[0, src].astype(F32)[:NL], halo_in[1, src].astype(F32)[:NL])
        added.append(pltpu.roll(edges, 64, 1) * 0.5)
        x_s[pl.ds(NL * src, NL), :] = pre_in[src].astype(F32)[:NL] + added[src]
    h_s[:LEVELS, :] = layers(x_s[:LEVELS, :])
    day = fl_s[pl.ds(0, 1), pl.ds(0, 128)]
    for dst in range(LEV):
        small_s[pl.ds(SMALL * dst, NL), :] = added[dst] + h_s[pl.ds(NL * dst, NL), :] * day
    late_out[...] = small_s[...].astype(BF16).reshape(LEV, SMALL, 128)
    late_copies = exchange(late_out, late_in, late_send, late_recv)
    for part in range(4):
        for copy in heat_copies[part]:
            copy.wait_recv()
        if part < 3:
            unpack(part, None)
    accumulate(1, 4, t_v)
    for copy in late_copies:
        copy.wait_recv()
    unpack(3, [late_in[j].astype(F32)[:NL] for j in range(4)])
    accumulate(0, 1, out_v)

    for copies in halo_copies + col_copies + heat_copies + [pre_copies, late_copies]:
        for copy in copies:
            copy.wait_send()


def on_device(t, u, v, pos, sunlit, w0, b0, wi, bi, wr):
    shape = t.shape
    args = [
        t.reshape(ROWS, NE), u.reshape(ROWS, NE), v.reshape(ROWS, NE), pos, sunlit.reshape(1, NE),
        jnp.asarray(derivative_blocks()), w0.T, b0.reshape(1, UNITS), wi.reshape(2 * UNITS, UNITS),
        bi, wr,
    ]
    vmem = [pltpu.VMEM(a.shape, a.dtype) for a in args]
    dma = pltpu.SemaphoreType.DMA
    scratch = vmem + [
        pltpu.VMEM((NE, NE), BF16),
        pltpu.VMEM((4, ROWS, 128), F32),
        pltpu.VMEM((4, ROWS, 128), F32),
        pltpu.VMEM((4, NODES, 24, 128), F32),
        pltpu.VMEM((8, NE), F32),
        pltpu.VMEM((UNITS, 128), BF16),
        pltpu.VMEM((2 * UNITS, UNITS), BF16),
        pltpu.VMEM((2, UNITS, 128), F32),
        pltpu.VMEM((LEV * SMALL, 128), F32),
        pltpu.VMEM((LEV, SMALL, 128), BF16),
        pltpu.VMEM((2, LEV, SMALL, 128), BF16),
    ]
    scratch += [pltpu.VMEM((LEV, SMALL, 128), BF16)] * 4
    scratch += [
        pltpu.VMEM((LEV * TALL, 128), F32),
        pltpu.VMEM((ROWS, 128), F32),
        pltpu.VMEM((ROWS, 128), F32),
        pltpu.VMEM((TALL, 128), F32),
        pltpu.VMEM((4, ROWS, 128), F32),
    ]
    scratch += [pltpu.VMEM((4, LEV, TALL, 128), BF16)] * 4
    scratch += [
        dma((len(args),)), pltpu.SemaphoreType.REGULAR, dma((2, LEV)), dma((2, LEV)),
        dma((4, 3)), dma((4, 3)), dma((4, 3)), dma((4, 3)),
        dma((3,)), dma((3,)), dma((3,)), dma((3,)),
    ]
    any_spec = pl.BlockSpec(memory_space=pltpu.HBM)
    out = pl.pallas_call(
        kernel,
        out_shape=pltpu.VMEM((ROWS, NE), F32),
        in_specs=[any_spec] * len(args),
        out_specs=pl.BlockSpec(memory_space=pltpu.VMEM),
        scratch_shapes=scratch,
        compiler_params=pltpu.CompilerParams(
            collective_id=0, has_side_effects=True, vmem_limit_bytes=60 * 2**20
        ),
        name="section",
    )(*args)
    return out.reshape(shape)


def solution(mesh):
    in_specs = (
        P("lev", None, "elem"), P("lev", None, "elem"), P("lev", None, "elem"), P("elem", None),
        P("elem"), P(), P(), P(), P(), P(),
    )
    out_specs = P("lev", None, "elem")
    return jax.shard_map(
        on_device, mesh=mesh, in_specs=in_specs, out_specs=out_specs, check_vma=False
    )
```

time: 30.4 us -> 25.2 us (0.83)
  Pallas kernels: 29.4 us -> 24.2 us
    pallas_call x1, Pallas kernels: 29.4 us -> 24.2 us  [on_device(): pl.pallas_call(kernel, out_shape=pltpu.VMEM((ROWS, NE), F32), in_specs=[a...]
where the time goes in v3:
time: 25.2 us; the launch traced here: 25.1 us
  Pallas kernels  24.2 us (96%)
  local copies, waits for them, and re-layouts  0.82 us (3%)
    pallas_call x1, Pallas kernels, on_device(): pl.pallas_call(kernel, out_shape=pltpu.VMEM((ROWS, NE), F32), in_specs=[a...  24.2 us
    unnamed x1, local copies, waits for them, and re-layouts  0.82 us

profile of v3, /device:TPU:1, one launch (start us, length us, event | category | flops | bytes accessed | tf_op | source)
XLA Modules:
  0.0 25.1 jit_solution(13226388948082126188)
XLA Ops:
  0.0 24.2 %section.1 = f32[288,512]{1,0:T(8,128)S(1)} custom-call(f32[288,512]{1,0:T(8,128)} %bitcast.10, bf16[288,512]{1,0:T(8,128)(2,1)} %bitcast.11, bf16[288,512]{1,0:T(8,128)(2,1)} %bitcast.12, s32[1,512]{1,0:T(1,128)} %pos_hbm.1, s32[1,512]{1,0:T(1,128)} %bitcast.14, f32[144,48]{1,0:T(8,128)} %constant.2.clone.d_hbm, bf16[72,512]{1,0:T(8,128)(2,1)} %bitcast.13, ...), custom_call_target="tpu_custom_call" | custom-call | tf_op jit(solution)/shard_map/section/pallas_call | solution.py:357
  24.2 0.8 %copy.13 = f32[18,16,512]{2,1,0:T(8,128)} copy(f32[18,16,512]{2,1,0:T(8,128)S(1)} %bitcast.8) | data formatting | bytes 1179648

commit v4 on v3

--- a/solution.py
+++ b/solution.py
@@ -18,9 +18,9 @@
 ROWS = NL * NODES
 NE = 512
 BLOCK = 48
-CHUNKS = (2, 3, 1, 0)
-TALL = 80
-SMALL = 32
+PARTS = ((2,), (3, 1), (0,))
+TALL = (80, 144, 80)
+EDGE = 48
 LEVELS = NL * LEV
 UNITS = 512
 NT = (((1,), (1,)), ((), ()))
@@ -58,11 +58,14 @@
     out_v,
     t_v, u_v, v_v, pos_v, flag_v, d_v, w0_v, b0_v, wi_v, bi_v, wr_v,
     q_s, tg_s, ag_s, dd_s, fl_s, w0_s, wi_s, bias_s,
-    small_s, halo_out, halo_in, pre_out, pre_in, late_out, late_in, col_s, x_s, h_s, hin_s, sum_s,
-    col_out, col_in, heat_out, heat_in,
+    edge_s, halo_out, halo_in, pre_out, pre_in, add_s, col_s, x_s, h_s, hin_s, sum_s,
+    col_out0, col_out1, col_out2, col_in0, col_in1, col_in2,
+    heat_out0, heat_out1, heat_out2, heat_in0, heat_in1, heat_in2,
     in_sem, ready, halo_send, halo_recv, col_send, col_recv, heat_send, heat_recv,
-    pre_send, pre_recv, late_send, late_recv,
+    pre_send, pre_recv,
 ):
+    col_out, col_in = (col_out0, col_out1, col_out2), (col_in0, col_in1, col_in2)
+    heat_out, heat_in = (heat_out0, heat_out1, heat_out2), (heat_in0, heat_in1, heat_in2)
     me = lax.axis_index("lev")
     elem = lax.axis_index("elem")
     count = lax.axis_size("elem")
@@ -71,14 +74,16 @@
     peers = [lax.rem(me + d, LEV) for d in (2, 1, 3)]
 
     loads = {}
-    pairs = [
-        ("pos", pos_hbm, pos_v), ("t", t_hbm, t_v), ("d", d_hbm, d_v), ("u", u_hbm, u_v),
-        ("v", v_hbm, v_v), ("flag", flag_hbm, flag_v), ("w0", w0_hbm, w0_v), ("b0", b0_hbm, b0_v),
-        ("bi", bi_hbm, bi_v), ("wi", wi_hbm, wi_v), ("wr", wr_hbm, wr_v),
-    ]
-    for n, (name, src, dst) in enumerate(pairs):
-        loads[name] = pltpu.make_async_copy(src, dst, in_sem.at[n])
-        loads[name].start()
+
+    def start(first, pairs):
+        for n, (name, src, dst) in enumerate(pairs):
+            loads[name] = pltpu.make_async_copy(src, dst, in_sem.at[first + n])
+            loads[name].start()
+
+    start(0, [
+        ("pos", pos_hbm, pos_v), ("t", t_hbm, t_v), ("u", u_hbm, u_v), ("v", v_hbm, v_v),
+        ("d", d_hbm, d_v),
+    ])
 
     barrier = pltpu.get_barrier_semaphore()
     for p in peers:
@@ -126,16 +131,18 @@
     edge = {(i, j): node(i, j, 0) for i in (0, 3) for j in range(4)}
     along_second(edge, 0)
     along_second(edge, 3)
-    small_s[...] = jnp.zeros(small_s.shape, F32)
-    for j in range(4):
-        small_s[pl.ds(SMALL * j, NL), :] = jnp.where(left, edge[3, j], edge[0, j])
-    halo_out[...] = small_s[...].astype(BF16).reshape(LEV, SMALL, 128)
+    edge_s[...] = jnp.zeros(edge_s.shape, F32)
+    for h in range(2):
+        even, odd = 2 * h, 2 * h + 1
+        edge_s[0, pl.ds(24 * h, NL), :] = jnp.where(left, edge[3, even], pltpu.roll(edge[3, odd], 64, 1))
+        edge_s[1, pl.ds(24 * h, NL), :] = jnp.where(left, pltpu.roll(edge[0, even], 64, 1), edge[0, odd])
+    halo_out[...] = edge_s[...].astype(BF16)
     pl.semaphore_wait(barrier, 7)
     targets = [lax.rem(me + d, LEV) for d in range(LEV)]
     halo_copies = [
         [
             pltpu.make_async_remote_copy(
-                src_ref=halo_out.at[q], dst_ref=halo_in.at[n, me], send_sem=halo_send.at[n, d],
+                src_ref=halo_out.at[n], dst_ref=halo_in.at[n, me], send_sem=halo_send.at[n, d],
                 recv_sem=halo_recv.at[n, d], device_id=(e, q), device_id_type=MESH,
             )
             for d, q in enumerate(targets)
@@ -147,6 +154,11 @@
     for q in targets:
         pl.semaphore_signal(ready, inc=1, device_id=(nxt, q), device_id_type=MESH)
 
+    start(5, [
+        ("flag", flag_hbm, flag_v), ("w0", w0_hbm, w0_v), ("b0", b0_hbm, b0_v),
+        ("bi", bi_hbm, bi_v), ("wi", wi_hbm, wi_v), ("wr", wr_hbm, wr_v),
+    ])
+
     def send_back():
         pl.semaphore_wait(ready, LEV)
         for copy in halo_copies[1]:
@@ -158,16 +170,21 @@
     loads.pop("flag").wait()
     flags = jnp.broadcast_to(flag_v[...].astype(F32), (16, NE)).astype(BF16)
     t_lo = (t_v[...] - t_hi.astype(F32)).astype(BF16)
-    both = lax.dot_general(
-        jnp.concatenate([t_hi, t_lo, flags], axis=0), q_s[...], NT, preferred_element_type=F32
-    )
-    for c in range(4):
-        lanes = slice(128 * c, 128 * c + 128)
-        ag_s[c] = both[:ROWS, lanes] + both[ROWS : 2 * ROWS, lanes]
-    fl_s[...] = both[2 * ROWS : 2 * ROWS + 8]
-
-    def dss(part):
-        c = CHUNKS[part]
+    stack = jnp.concatenate([t_hi, t_lo, flags], axis=0)
+
+    def to_slots(first):
+        both = lax.dot_general(
+            stack, q_s[128 * first : 128 * first + 256, :], NT, preferred_element_type=F32
+        )
+        for h in range(2):
+            lanes = slice(128 * h, 128 * h + 128)
+            ag_s[first + h] = both[:ROWS, lanes] + both[ROWS : 2 * ROWS, lanes]
+        fl_s[:, pl.ds(128 * first, 256)] = both[2 * ROWS : 2 * ROWS + 8]
+
+    to_slots(2)
+
+    def dss(part, h):
+        c = PARTS[part][h]
         t = {(i, j): node(i, j, c) for i in range(4) for j in range(4)}
         for j in range(4):
             own0, own3 = t[0, j], t[3, j]
@@ -186,7 +203,7 @@
                 p = 4 * i + j
                 dd_s[c, p, :NL, :] = t[i, j]
                 col[i, j] = ag_s[c, pl.ds(p, NL, stride=NODES), :] + t[i, j]
-                col_s[pl.ds(TALL * i + j, NL, stride=4), :] = col[i, j]
+                col_s[pl.ds(TALL[part] * i + 72 * h + j, NL, stride=4), :] = col[i, j]
         return col
 
     def exchange(out, into, send, recv):
@@ -202,12 +219,12 @@
         return copies
 
     def send_columns(part):
-        for i in range(LEV):
-            col_s[pl.ds(TALL * i + 72, 8), :] = jnp.zeros((8, 128), F32)
-        col_out[part] = col_s[...].astype(BF16).reshape(LEV, TALL, 128)
-        return exchange(
-            col_out.at[part], col_in.at[part], col_send.at[part], col_recv.at[part]
-        )
+        tall, used = TALL[part], 72 * len(PARTS[part])
+        if tall > used:
+            for i in range(LEV):
+                col_s[pl.ds(tall * i + used, tall - used), :] = jnp.zeros((tall - used, 128), F32)
+        col_out[part][...] = col_s[: LEV * tall, :].astype(BF16).reshape(LEV, tall, 128)
+        return exchange(col_out[part], col_in[part], col_send.at[part], col_recv.at[part])
 
     def gate(h):
         return (h + h * jnp.tanh(h)).astype(BF16)
@@ -223,49 +240,60 @@
         return jnp.dot(wr_v[...], hid, preferred_element_type=F32)
 
     def network(part, copies):
+        size = len(PARTS[part])
         for copy in copies:
             copy.wait_recv()
         for src in range(LEV):
-            x_s[pl.ds(72 * src, 72), :] = col_in[part, src].astype(F32)[:72]
-        x = jnp.concatenate([x_s[pl.ds(j, LEVELS, stride=4), :] for j in range(4)], axis=1)
-        heat = layers(x)
-        for j in range(4):
-            h_s[pl.ds(j, LEVELS, stride=4), :] = heat[:, 128 * j : 128 * j + 128]
-        pad = jnp.zeros((8, 128), F32)
+            block = col_in[part][src].astype(F32)
+            for h in range(size):
+                x_s[pl.ds(288 * h + 72 * src, 72), :] = block[72 * h : 72 * h + 72]
+        heat = layers(jnp.concatenate(
+            [x_s[pl.ds(288 * h + j, LEVELS, stride=4), :] for j in range(4) for h in range(size)], axis=1
+        ))
+        for n in range(4 * size):
+            j, h = divmod(n, size)
+            h_s[pl.ds(288 * h + j, LEVELS, stride=4), :] = heat[:, 128 * n : 128 * n + 128]
         for dst in range(LEV):
-            block = jnp.concatenate([h_s[pl.ds(72 * dst, 72), :], pad], axis=0)
-            heat_out[part, dst] = block.astype(BF16)
-        return exchange(
-            heat_out.at[part], heat_in.at[part], heat_send.at[part], heat_recv.at[part]
+            block = [h_s[pl.ds(288 * h + 72 * dst, 72), :] for h in range(size)]
+            if size == 1:
+                block.append(jnp.zeros((8, 128), F32))
+            heat_out[part][dst] = jnp.concatenate(block, axis=0).astype(BF16)
+        return exchange(heat_out[part], heat_in[part], heat_send.at[part], heat_recv.at[part])
+
+    def unpack(part, late):
+        for q in range(LEV):
+            hin_s[: TALL[part], :] = heat_in[part][q].astype(F32)
+            for h, c in enumerate(PARTS[part]):
+                day = fl_s[pl.ds(0, 1), pl.ds(128 * c, 128)]
+                for j in range(4):
+                    p = 4 * q + j
+                    heat = hin_s[pl.ds(72 * h + j, NL, stride=4), :] * day
+                    if c == 0 and q == 0:
+                        heat = jnp.where(left, heat, late[j])
+                    if c == 0 and q == 3:
+                        heat = jnp.where(left, late[j], heat)
+                    sum_s[c, pl.ds(p, NL, stride=NODES), :] = dd_s[c, p, :NL, :] + heat
+
+    col_copies = []
+    for part, chunks in enumerate(PARTS):
+        for h in range(len(chunks)):
+            col = dss(part, h)
+        col_copies.append(send_columns(part))
+        if part == 0:
+            to_slots(0)
+    col_s[pl.ds(72, 8), :] = jnp.zeros((8, 128), F32)
+    for j in range(4):
+        col_s[pl.ds(j, NL, stride=4), :] = jnp.where(left, col[3, j], col[0, j])
+    pre_out[...] = col_s[:80, :].astype(BF16)
+    pre_copies = []
+    for n, p in enumerate(peers):
+        copy = pltpu.make_async_remote_copy(
+            src_ref=pre_out, dst_ref=pre_in.at[me], send_sem=pre_send.at[n],
+            recv_sem=pre_recv.at[n], device_id=(elem, p), device_id_type=MESH,
         )
-
-    def unpack(part, late):
-        c = CHUNKS[part]
-        day = fl_s[pl.ds(0, 1), pl.ds(128 * c, 128)]
-        for q in range(LEV):
-            hin_s[...] = heat_in[part, q].astype(F32)
-            for j in range(4):
-                p = 4 * q + j
-                heat = hin_s[pl.ds(j, NL, stride=4), :] * day
-                if late is not None and q == 0:
-                    heat = jnp.where(left, heat, late[j])
-                if late is not None and q == 3:
-                    heat = jnp.where(left, late[j], heat)
-                sum_s[c, pl.ds(p, NL, stride=NODES), :] = dd_s[c, p, :NL, :] + heat
-
-    def accumulate(first, last, base):
-        total = jnp.concatenate([sum_s[c] for c in range(first, last)], axis=1).astype(BF16)
-        rows = q_s[128 * first : 128 * last, :]
-        out_v[...] = base[...] + jnp.dot(total, rows, preferred_element_type=F32)
-
-    col_copies = []
-    for part in range(4):
-        col = dss(part)
-        col_copies.append(send_columns(part))
-    for j in range(4):
-        small_s[pl.ds(SMALL * j, NL), :] = jnp.where(left, col[3, j], col[0, j])
-    pre_out[...] = small_s[...].astype(BF16).reshape(LEV, SMALL, 128)
-    pre_copies = exchange(pre_out, pre_in, pre_send, pre_recv)
+        copy.start()
+        pre_copies.append(copy)
+    pre_in[me] = pre_out[...]
     closing = lax.rem(elem, count // 2) == 0
     pl.when(jnp.logical_not(closing))(send_back)
 
@@ -286,33 +314,46 @@
     wi_s[...] = wi_v[...] * jnp.asarray(0.5, BF16)
     loads.pop("wr").wait()
 
-    heat_copies = [network(part, col_copies[part]) for part in range(4)]
+    heat_copies = [network(part, copies) for part, copies in enumerate(col_copies)]
+
     pl.when(closing)(send_back)
-    for copy in halo_copies[0] + halo_copies[1] + pre_copies:
+    for copy in pre_copies:
         copy.wait_recv()
-    added = []
     for src in range(LEV):
-        edges = jnp.where(left, halo_in[0, src].astype(F32)[:NL], halo_in[1, src].astype(F32)[:NL])
-        added.append(pltpu.roll(edges, 64, 1) * 0.5)
-        x_s[pl.ds(NL * src, NL), :] = pre_in[src].astype(F32)[:NL] + added[src]
-    h_s[:LEVELS, :] = layers(x_s[:LEVELS, :])
+        x_s[pl.ds(72 * src, 72), :] = pre_in[src].astype(F32)[:72]
+    for copy in halo_copies[0] + halo_copies[1]:
+        copy.wait_recv()
+    for src in range(LEV):
+        below, above = halo_in[0, src].astype(F32), halo_in[1, src].astype(F32)
+        for j in range(4):
+            row = 24 * (j // 2)
+            before, after = below[row : row + NL], above[row : row + NL]
+            if j % 2 == 0:
+                before = pltpu.roll(before, 64, 1)
+            else:
+                after = pltpu.roll(after, 64, 1)
+            rows = pl.ds(72 * src + j, NL, stride=4)
+            add = jnp.where(left, after, before) * 0.5
+            add_s[rows, :] = add
+            x_s[rows, :] = x_s[rows, :] + add
+    heat = layers(
+        jnp.concatenate([x_s[pl.ds(j, LEVELS, stride=4), :] for j in range(4)], axis=1)
+    )
+    for j in range(4):
+        h_s[pl.ds(j, LEVELS, stride=4), :] = heat[:, 128 * j : 128 * j + 128]
     day = fl_s[pl.ds(0, 1), pl.ds(0, 128)]
-    for dst in range(LEV):
-        small_s[pl.ds(SMALL * dst, NL), :] = added[dst] + h_s[pl.ds(NL * dst, NL), :] * day
-    late_out[...] = small_s[...].astype(BF16).reshape(LEV, SMALL, 128)
-    late_copies = exchange(late_out, late_in, late_send, late_recv)
-    for part in range(4):
+    late = []
+    for j in range(4):
+        rows = pl.ds(72 * me + j, NL, stride=4)
+        late.append(add_s[rows, :] + h_s[rows, :] * day)
+    for part in range(len(PARTS)):
         for copy in heat_copies[part]:
             copy.wait_recv()
-        if part < 3:
-            unpack(part, None)
-    accumulate(1, 4, t_v)
-    for copy in late_copies:
-        copy.wait_recv()
-    unpack(3, [late_in[j].astype(F32)[:NL] for j in range(4)])
-    accumulate(0, 1, out_v)
-
-    for copies in halo_copies + col_copies + heat_copies + [pre_copies, late_copies]:
+        unpack(part, late)
+    total = jnp.concatenate([sum_s[c] for c in range(4)], axis=1).astype(BF16)
+    out_v[...] = t_v[...] + jnp.dot(total, q_s[...], preferred_element_type=F32)
+
+    for copies in halo_copies + col_copies + heat_copies + [pre_copies]:
         for copy in copies:
             copy.wait_send()
 
@@ -335,23 +376,22 @@
         pltpu.VMEM((UNITS, 128), BF16),
         pltpu.VMEM((2 * UNITS, UNITS), BF16),
         pltpu.VMEM((2, UNITS, 128), F32),
-        pltpu.VMEM((LEV * SMALL, 128), F32),
-        pltpu.VMEM((LEV, SMALL, 128), BF16),
-        pltpu.VMEM((2, LEV, SMALL, 128), BF16),
-    ]
-    scratch += [pltpu.VMEM((LEV, SMALL, 128), BF16)] * 4
-    scratch += [
-        pltpu.VMEM((LEV * TALL, 128), F32),
+        pltpu.VMEM((2, EDGE, 128), F32),
+        pltpu.VMEM((2, EDGE, 128), BF16),
+        pltpu.VMEM((2, LEV, EDGE, 128), BF16),
+        pltpu.VMEM((80, 128), BF16),
+        pltpu.VMEM((LEV, 80, 128), BF16),
         pltpu.VMEM((ROWS, 128), F32),
-        pltpu.VMEM((ROWS, 128), F32),
-        pltpu.VMEM((TALL, 128), F32),
+        pltpu.VMEM((LEV * max(TALL), 128), F32),
+        pltpu.VMEM((2 * ROWS, 128), F32),
+        pltpu.VMEM((2 * ROWS, 128), F32),
+        pltpu.VMEM((max(TALL), 128), F32),
         pltpu.VMEM((4, ROWS, 128), F32),
     ]
-    scratch += [pltpu.VMEM((4, LEV, TALL, 128), BF16)] * 4
+    scratch += [pltpu.VMEM((LEV, tall, 128), BF16) for _ in range(4) for tall in TALL]
     scratch += [
         dma((len(args),)), pltpu.SemaphoreType.REGULAR, dma((2, LEV)), dma((2, LEV)),
-        dma((4, 3)), dma((4, 3)), dma((4, 3)), dma((4, 3)),
-        dma((3,)), dma((3,)), dma((3,)), dma((3,)),
+        dma((3, 3)), dma((3, 3)), dma((3, 3)), dma((3, 3)), dma((3,)), dma((3,)),
     ]
     any_spec = pl.BlockSpec(memory_space=pltpu.HBM)
     out = pl.pallas_call(

time: 25.2 us -> 23.5 us (0.933)
  Pallas kernels: 24.2 us -> 22.5 us
    pallas_call x1, Pallas kernels: 24.2 us -> 22.5 us  [on_device(): pl.pallas_call(kernel, out_shape=pltpu.VMEM((ROWS, NE), F32), in_specs=[a...]
where the time goes in v4:
time: 23.5 us; the launch traced here: 23.4 us
  Pallas kernels  22.5 us (96%)
  local copies, waits for them, and re-layouts  0.82 us (3%)
    pallas_call x1, Pallas kernels, on_device(): pl.pallas_call(kernel, out_shape=pltpu.VMEM((ROWS, NE), F32), in_specs=[a...  22.5 us
    unnamed x1, local copies, waits for them, and re-layouts  0.82 us

profile of v4, /device:TPU:1, one launch (start us, length us, event | category | flops | bytes accessed | tf_op | source)
XLA Modules:
  0.0 23.4 jit_solution(14941846691922029139)
XLA Ops:
  0.0 22.5 %section.1 = f32[288,512]{1,0:T(8,128)S(1)} custom-call(f32[288,512]{1,0:T(8,128)} %bitcast.10, bf16[288,512]{1,0:T(8,128)(2,1)} %bitcast.11, bf16[288,512]{1,0:T(8,128)(2,1)} %bitcast.12, s32[1,512]{1,0:T(1,128)} %pos_hbm.1, s32[1,512]{1,0:T(1,128)} %bitcast.14, f32[144,48]{1,0:T(8,128)} %constant.2.clone.d_hbm, bf16[72,512]{1,0:T(8,128)(2,1)} %bitcast.13, ...), custom_call_target="tpu_custom_call" | custom-call | tf_op jit(solution)/shard_map/section/pallas_call | solution.py:397
  22.5 0.8 %copy.13 = f32[18,16,512]{2,1,0:T(8,128)} copy(f32[18,16,512]{2,1,0:T(8,128)S(1)} %bitcast.8) | data formatting | bytes 1179648

commit v5 on v4

--- a/solution.py
+++ b/solution.py
@@ -18,6 +18,7 @@
 ROWS = NL * NODES
 NE = 512
 BLOCK = 48
+TALLER = 24 * NODES
 PARTS = ((2,), (3, 1), (0,))
 TALL = (80, 144, 80)
 EDGE = 48
@@ -82,7 +83,7 @@
 
     start(0, [
         ("pos", pos_hbm, pos_v), ("t", t_hbm, t_v), ("u", u_hbm, u_v), ("v", v_hbm, v_v),
-        ("d", d_hbm, d_v),
+        ("d", d_hbm, d_v), ("flag", flag_hbm, flag_v),
     ])
 
     barrier = pltpu.get_barrier_semaphore()
@@ -112,7 +113,7 @@
         tend = g[2 * BLOCK :] - u * g[:BLOCK] - v * g[BLOCK : 2 * BLOCK]
         parts.append(tend.astype(BF16))
     tend = jnp.concatenate(parts, axis=0)
-    tg_s[0] = lax.dot_general(tend, q_s[:128, :], NT, preferred_element_type=F32)
+    tg_s[0, :ROWS] = lax.dot_general(tend, q_s[:128, :], NT, preferred_element_type=F32)
 
     lane = lax.broadcasted_iota(jnp.int32, (NL, 128), 1)
     left = lane < 64
@@ -151,13 +152,7 @@
     ]
     for copy in halo_copies[0]:
         copy.start()
-    for q in targets:
-        pl.semaphore_signal(ready, inc=1, device_id=(nxt, q), device_id_type=MESH)
-
-    start(5, [
-        ("flag", flag_hbm, flag_v), ("w0", w0_hbm, w0_v), ("b0", b0_hbm, b0_v),
-        ("bi", bi_hbm, bi_v), ("wi", wi_hbm, wi_v), ("wr", wr_hbm, wr_v),
-    ])
+
 
     def send_back():
         pl.semaphore_wait(ready, LEV)
@@ -166,7 +161,7 @@
 
     rest = lax.dot_general(tend, q_s[128:, :], NT, preferred_element_type=F32)
     for c in range(1, 4):
-        tg_s[c] = rest[:, 128 * (c - 1) : 128 * c]
+        tg_s[c, :ROWS] = rest[:, 128 * (c - 1) : 128 * c]
     loads.pop("flag").wait()
     flags = jnp.broadcast_to(flag_v[...].astype(F32), (16, NE)).astype(BF16)
     t_lo = (t_v[...] - t_hi.astype(F32)).astype(BF16)
@@ -178,7 +173,7 @@
         )
         for h in range(2):
             lanes = slice(128 * h, 128 * h + 128)
-            ag_s[first + h] = both[:ROWS, lanes] + both[ROWS : 2 * ROWS, lanes]
+            ag_s[first + h, :ROWS] = both[:ROWS, lanes] + both[ROWS : 2 * ROWS, lanes]
         fl_s[:, pl.ds(128 * first, 256)] = both[2 * ROWS : 2 * ROWS + 8]
 
     to_slots(2)
@@ -280,6 +275,12 @@
             col = dss(part, h)
         col_copies.append(send_columns(part))
         if part == 0:
+            start(6, [
+                ("w0", w0_hbm, w0_v), ("b0", b0_hbm, b0_v), ("bi", bi_hbm, bi_v),
+                ("wi", wi_hbm, wi_v), ("wr", wr_hbm, wr_v),
+            ])
+            for q in targets:
+                pl.semaphore_signal(ready, inc=1, device_id=(nxt, q), device_id_type=MESH)
             to_slots(0)
     col_s[pl.ds(72, 8), :] = jnp.zeros((8, 128), F32)
     for j in range(4):
@@ -295,7 +296,6 @@
         pre_copies.append(copy)
     pre_in[me] = pre_out[...]
     closing = lax.rem(elem, count // 2) == 0
-    pl.when(jnp.logical_not(closing))(send_back)
 
     loads.pop("w0").wait()
     loads.pop("b0").wait()
@@ -314,6 +314,7 @@
     wi_s[...] = wi_v[...] * jnp.asarray(0.5, BF16)
     loads.pop("wr").wait()
 
+    pl.when(jnp.logical_not(closing))(send_back)
     heat_copies = [network(part, copies) for part, copies in enumerate(col_copies)]
 
     pl.when(closing)(send_back)
@@ -346,12 +347,18 @@
     for j in range(4):
         rows = pl.ds(72 * me + j, NL, stride=4)
         late.append(add_s[rows, :] + h_s[rows, :] * day)
+    def accumulate(first, last, base):
+        total = jnp.concatenate([sum_s[c, :ROWS] for c in range(first, last)], axis=1).astype(BF16)
+        rows = q_s[128 * first : 128 * last, :]
+        out_v[...] = base[...] + jnp.dot(total, rows, preferred_element_type=F32)
+
     for part in range(len(PARTS)):
         for copy in heat_copies[part]:
             copy.wait_recv()
         unpack(part, late)
-    total = jnp.concatenate([sum_s[c] for c in range(4)], axis=1).astype(BF16)
-    out_v[...] = t_v[...] + jnp.dot(total, q_s[...], preferred_element_type=F32)
+        if part == 1:
+            accumulate(1, 4, t_v)
+    accumulate(0, 1, out_v)
 
     for copies in halo_copies + col_copies + heat_copies + [pre_copies]:
         for copy in copies:
@@ -369,8 +376,8 @@
     dma = pltpu.SemaphoreType.DMA
     scratch = vmem + [
         pltpu.VMEM((NE, NE), BF16),
-        pltpu.VMEM((4, ROWS, 128), F32),
-        pltpu.VMEM((4, ROWS, 128), F32),
+        pltpu.VMEM((4, TALLER, 128), F32),
+        pltpu.VMEM((4, TALLER, 128), F32),
         pltpu.VMEM((4, NODES, 24, 128), F32),
         pltpu.VMEM((8, NE), F32),
         pltpu.VMEM((UNITS, 128), BF16),
@@ -381,12 +388,12 @@
         pltpu.VMEM((2, LEV, EDGE, 128), BF16),
         pltpu.VMEM((80, 128), BF16),
         pltpu.VMEM((LEV, 80, 128), BF16),
-        pltpu.VMEM((ROWS, 128), F32),
-        pltpu.VMEM((LEV * max(TALL), 128), F32),
-        pltpu.VMEM((2 * ROWS, 128), F32),
-        pltpu.VMEM((2 * ROWS, 128), F32),
-        pltpu.VMEM((max(TALL), 128), F32),
-        pltpu.VMEM((4, ROWS, 128), F32),
+        pltpu.VMEM((ROWS + 32, 128), F32),
+        pltpu.VMEM((LEV * max(TALL) + 32, 128), F32),
+        pltpu.VMEM((2 * ROWS + 32, 128), F32),
+        pltpu.VMEM((2 * ROWS + 32, 128), F32),
+        pltpu.VMEM((max(TALL) + 32, 128), F32),
+        pltpu.VMEM((4, TALLER, 128), F32),
     ]
     scratch += [pltpu.VMEM((LEV, tall, 128), BF16) for _ in range(4) for tall in TALL]
     scratch += [

time: 23.5 us -> 23.6 us (level)
  no operation moved by 1% of the time
where the time goes in v5:
time: 23.6 us; the launch traced here: 23.5 us
  Pallas kernels  22.6 us (96%)
  local copies, waits for them, and re-layouts  0.82 us (3%)
    pallas_call x1, Pallas kernels, on_device(): pl.pallas_call(kernel, out_shape=pltpu.VMEM((ROWS, NE), F32), in_specs=[a...  22.6 us
    unnamed x1, local copies, waits for them, and re-layouts  0.82 us

profile of v5, /device:TPU:1, one launch (start us, length us, event | category | flops | bytes accessed | tf_op | source)
XLA Modules:
  0.0 23.5 jit_solution(7301835218800236983)
XLA Ops:
  0.0 22.6 %section.1 = f32[288,512]{1,0:T(8,128)S(1)} custom-call(f32[288,512]{1,0:T(8,128)} %bitcast.10, bf16[288,512]{1,0:T(8,128)(2,1)} %bitcast.11, bf16[288,512]{1,0:T(8,128)(2,1)} %bitcast.12, s32[1,512]{1,0:T(1,128)} %pos_hbm.1, s32[1,512]{1,0:T(1,128)} %bitcast.14, f32[144,48]{1,0:T(8,128)} %constant.2.clone.d_hbm, bf16[72,512]{1,0:T(8,128)(2,1)} %bitcast.13, ...), custom_call_target="tpu_custom_call" | custom-call | tf_op jit(solution)/shard_map/section/pallas_call | solution.py:404
  22.6 0.8 %copy.13 = f32[18,16,512]{2,1,0:T(8,128)} copy(f32[18,16,512]{2,1,0:T(8,128)S(1)} %bitcast.8) | data formatting | bytes 1179648

commit v6 on v5

--- a/solution.py
+++ b/solution.py
@@ -19,8 +19,8 @@
 NE = 512
 BLOCK = 48
 TALLER = 24 * NODES
-PARTS = ((2,), (3, 1), (0,))
-TALL = (80, 144, 80)
+PARTS = ((2, 3), (1,), (0,))
+TALL = (144, 80, 80)
 EDGE = 48
 LEVELS = NL * LEV
 UNITS = 512
@@ -317,6 +317,19 @@
     pl.when(jnp.logical_not(closing))(send_back)
     heat_copies = [network(part, copies) for part, copies in enumerate(col_copies)]
 
+    def accumulate(first, last, base):
+        total = jnp.concatenate([sum_s[c, :ROWS] for c in range(first, last)], axis=1).astype(BF16)
+        rows = q_s[128 * first : 128 * last, :]
+        out_v[...] = base[...] + jnp.dot(total, rows, preferred_element_type=F32)
+
+    def finish(part):
+        for copy in heat_copies[part]:
+            copy.wait_recv()
+        unpack(part, late)
+
+    late = []
+    finish(0)
+    accumulate(2, 4, t_v)
     pl.when(closing)(send_back)
     for copy in pre_copies:
         copy.wait_recv()
@@ -343,22 +356,12 @@
     for j in range(4):
         h_s[pl.ds(j, LEVELS, stride=4), :] = heat[:, 128 * j : 128 * j + 128]
     day = fl_s[pl.ds(0, 1), pl.ds(0, 128)]
-    late = []
     for j in range(4):
         rows = pl.ds(72 * me + j, NL, stride=4)
         late.append(add_s[rows, :] + h_s[rows, :] * day)
-    def accumulate(first, last, base):
-        total = jnp.concatenate([sum_s[c, :ROWS] for c in range(first, last)], axis=1).astype(BF16)
-        rows = q_s[128 * first : 128 * last, :]
-        out_v[...] = base[...] + jnp.dot(total, rows, preferred_element_type=F32)
-
-    for part in range(len(PARTS)):
-        for copy in heat_copies[part]:
-            copy.wait_recv()
-        unpack(part, late)
-        if part == 1:
-            accumulate(1, 4, t_v)
-    accumulate(0, 1, out_v)
+    finish(1)
+    finish(2)
+    accumulate(0, 2, out_v)
 
     for copies in halo_copies + col_copies + heat_copies + [pre_copies]:
         for copy in copies:

time: 23.6 us -> 23.3 us (0.987)
  Pallas kernels: 22.6 us -> 22.3 us
    pallas_call x1, Pallas kernels: 22.6 us -> 22.3 us  [on_device(): pl.pallas_call(kernel, out_shape=pltpu.VMEM((ROWS, NE), F32), in_specs=[a...]
where the time goes in v6:
time: 23.3 us; the launch traced here: 23.1 us
  Pallas kernels  22.3 us (96%)
  local copies, waits for them, and re-layouts  0.82 us (4%)
    pallas_call x1, Pallas kernels, on_device(): pl.pallas_call(kernel, out_shape=pltpu.VMEM((ROWS, NE), F32), in_specs=[a...  22.3 us
    unnamed x1, local copies, waits for them, and re-layouts  0.82 us

profile of v6, /device:TPU:1, one launch (start us, length us, event | category | flops | bytes accessed | tf_op | source)
XLA Modules:
  0.0 23.1 jit_solution(15490403485686869593)
XLA Ops:
  0.0 22.3 %section.1 = f32[288,512]{1,0:T(8,128)S(1)} custom-call(f32[288,512]{1,0:T(8,128)} %bitcast.10, bf16[288,512]{1,0:T(8,128)(2,1)} %bitcast.11, bf16[288,512]{1,0:T(8,128)(2,1)} %bitcast.12, s32[1,512]{1,0:T(1,128)} %pos_hbm.1, s32[1,512]{1,0:T(1,128)} %bitcast.14, f32[144,48]{1,0:T(8,128)} %constant.2.clone.d_hbm, bf16[72,512]{1,0:T(8,128)(2,1)} %bitcast.13, ...), custom_call_target="tpu_custom_call" | custom-call | tf_op jit(solution)/shard_map/section/pallas_call | solution.py:407
  22.3 0.8 %copy.13 = f32[18,16,512]{2,1,0:T(8,128)} copy(f32[18,16,512]{2,1,0:T(8,128)S(1)} %bitcast.8) | data formatting | bytes 1179648

commit v7 on v6

--- a/solution.py
+++ b/solution.py
@@ -329,7 +329,8 @@
 
     late = []
     finish(0)
-    accumulate(2, 4, t_v)
+    finish(1)
+    accumulate(1, 4, t_v)
     pl.when(closing)(send_back)
     for copy in pre_copies:
         copy.wait_recv()
@@ -359,9 +360,8 @@
     for j in range(4):
         rows = pl.ds(72 * me + j, NL, stride=4)
         late.append(add_s[rows, :] + h_s[rows, :] * day)
-    finish(1)
     finish(2)
-    accumulate(0, 2, out_v)
+    accumulate(0, 1, out_v)
 
     for copies in halo_copies + col_copies + heat_copies + [pre_copies]:
         for copy in copies:

time: 23.3 us -> 23.8 us (1.021)
  Pallas kernels: 22.3 us -> 22.8 us
    pallas_call x1, Pallas kernels: 22.3 us -> 22.8 us  [on_device(): pl.pallas_call(kernel, out_shape=pltpu.VMEM((ROWS, NE), F32), in_specs=[a...]
where the time goes in v7:
time: 23.8 us; the launch traced here: 23.6 us
  Pallas kernels  22.8 us (96%)
  local copies, waits for them, and re-layouts  0.82 us (3%)
    pallas_call x1, Pallas kernels, on_device(): pl.pallas_call(kernel, out_shape=pltpu.VMEM((ROWS, NE), F32), in_specs=[a...  22.8 us
    unnamed x1, local copies, waits for them, and re-layouts  0.82 us

profile of v7, /device:TPU:1, one launch (start us, length us, event | category | flops | bytes accessed | tf_op | source)
XLA Modules:
  0.0 23.6 jit_solution(2853908062129984710)
XLA Ops:
  0.0 22.8 %section.1 = f32[288,512]{1,0:T(8,128)S(1)} custom-call(f32[288,512]{1,0:T(8,128)} %bitcast.10, bf16[288,512]{1,0:T(8,128)(2,1)} %bitcast.11, bf16[288,512]{1,0:T(8,128)(2,1)} %bitcast.12, s32[1,512]{1,0:T(1,128)} %pos_hbm.1, s32[1,512]{1,0:T(1,128)} %bitcast.14, f32[144,48]{1,0:T(8,128)} %constant.2.clone.d_hbm, bf16[72,512]{1,0:T(8,128)(2,1)} %bitcast.13, ...), custom_call_target="tpu_custom_call" | custom-call | tf_op jit(solution)/shard_map/section/pallas_call | solution.py:407
  22.8 0.8 %copy.13 = f32[18,16,512]{2,1,0:T(8,128)} copy(f32[18,16,512]{2,1,0:T(8,128)S(1)} %bitcast.8) | data formatting | bytes 1179648
